TPU v7x, 256 devices: a whole 4x4x8 slice. The times are simulated.
256 devices in a mesh: gx: 8 (over y, core), gy: 32 (over z, x).
Axes of the slice: x: 4, y: 4, z: 8, core: 2. Of those that a mesh axis runs over, the one named last changes fastest.
Arguments:
- motion_cotangent: float32 [3, 128, 512, 512], P(None, 'gx', 'gy'), may hold values from -8 to 8
- scaled_warmth: float32 [128, 512, 512], P('gx', 'gy'), may hold values from 0 to 1
- yielding_flags: int32 [128, 512, 512], P('gx', 'gy'), may hold values 0 or 1
- printed_flags: int32 [128, 512, 512], P('gx', 'gy'), may hold values 0 or 1
- material_label: int32 [128, 512, 512], P('gx', 'gy'), may hold values from 0 to 3
- phase_rigidity: float32 [4], replicated, may hold values from 0.5 to 4
- phase_dilatation: float32 [4], replicated, may hold values from 0.5 to 2
- phase_diffusivity: float32 [4], replicated, may hold values from 0.2 to 1
Outputs:
- adjoint_displacement: float32 [3, 128, 512, 512], P(None, 'gx', 'gy')
- thermal_adjoint: float32 [128, 512, 512], P('gx', 'gy')
All inputs are finite; a program needn't handle non-finite values. No bound on the sum of `yielding_flags` or of `printed_flags` on one device may be relied on, other than what follows from the above.
Results may differ from a plain program's by a relative error of at most 0.0001.
Values sent between devices are 32-bit elements; how exact they have to be, the bound alone decides.
A program may use at most 64 MiB of HBM per device.

v0:
```python
import jax
import jax.numpy as jnp
from jax import lax
from jax.sharding import PartitionSpec as P

ITERS = 2


def with_halo(array, sides, width):
    for axis, dim in sides:
        count, length = (lax.axis_size(axis), array.shape[dim])
        up = [(i, (i + 1) % count) for i in range(count - 1)]
        down = [(j, i) for i, j in up]
        last = lax.slice_in_dim(array, length - width, length, axis=dim)
        leading = lax.slice_in_dim(array, 0, width, axis=dim)
        before = lax.ppermute(last, axis, up)
        after = lax.ppermute(leading, axis, down)
        array = jnp.concatenate([before, array, after], axis=dim)
    return array


def pad_depth(field):
    widths = [(0, 0)] * (field.ndim - 1) + [(1, 1)]
    return jnp.pad(field, widths)


def neighbours(padded):
    return [
        padded[..., 2:, 1:-1, 1:-1],
        padded[..., :-2, 1:-1, 1:-1],
        padded[..., 1:-1, 2:, 1:-1],
        padded[..., 1:-1, :-2, 1:-1],
        padded[..., 1:-1, 1:-1, 2:],
        padded[..., 1:-1, 1:-1, :-2],
    ]


def indexed_values(table, material_label):
    result = jnp.zeros(material_label.shape, jnp.float32)
    for index in range(table.shape[0]):
        result = result + jnp.where(material_label == index, table[index], 0.0)
    return result


def squares(residual):
    return lax.psum(jnp.sum(residual * residual), ("gx", "gy"))


def per_device(
    motion_cotangent,
    scaled_warmth,
    yielding_flags,
    printed_flags,
    material_label,
    phase_rigidity,
    phase_dilatation,
    phase_diffusivity,
):
    hooke_tensor = (
        indexed_values(phase_rigidity, material_label)
        * (1.0 - 0.7 * yielding_flags.astype(jnp.float32))
        * (0.05 + 0.95 * printed_flags.astype(jnp.float32))
    )
    conductance = indexed_values(phase_diffusivity, material_label)
    thermal_scaling = (
        indexed_values(phase_dilatation, material_label) * (0.5 + scaled_warmth) * hooke_tensor
    )
    stacked = jnp.stack([hooke_tensor, conductance])
    coef_pad = pad_depth(with_halo(stacked, (("gx", 1), ("gy", 2)), 1))
    weights = [0.5 * (hooke_tensor + other) for other in neighbours(coef_pad[0])]
    cond_near = neighbours(coef_pad[1])
    diagonal = 0.5 + sum(weights)
    solution = jnp.zeros_like(motion_cotangent)
    residual = motion_cotangent
    direction = motion_cotangent
    norm_now = squares(residual)
    for iteration in range(ITERS):
        operate_padded = pad_depth(with_halo(direction, (("gx", 1), ("gy", 2)), 1))
        total = diagonal * direction
        for weight, operate_other in zip(weights, neighbours(operate_padded)):
            total = total - weight * operate_other
        step_size = norm_now / lax.psum(jnp.sum(direction * total), ("gx", "gy"))
        solution = solution + step_size * direction
        residual = residual - step_size * total
        norm_next = squares(residual)
        direction = residual + norm_next / norm_now * direction
        norm_now = norm_next
    padded = pad_depth(with_halo(solution, (("gx", 1), ("gy", 2)), 1))
    flux_balance = padded[0, 2:, 1:-1, 1:-1] - padded[0, :-2, 1:-1, 1:-1]
    flux_balance = flux_balance + (padded[1, 1:-1, 2:, 1:-1] - padded[1, 1:-1, :-2, 1:-1])
    flux_balance = flux_balance + (padded[2, 1:-1, 1:-1, 2:] - padded[2, 1:-1, 1:-1, :-2])
    energy_input = -0.5 * thermal_scaling * flux_balance
    source_pad = pad_depth(with_halo(energy_input, (("gx", 0), ("gy", 1)), 1))
    change = jnp.zeros_like(energy_input)
    for other_c, other_s in zip(cond_near, neighbours(source_pad)):
        change = change + 0.5 * (conductance + other_c) * (other_s - energy_input)
    thermal = energy_input + 0.15 * change
    return (solution, thermal)


def solution(mesh):
    in_specs = (
        P(None, "gx", "gy", None),
        P("gx", "gy", None),
        P("gx", "gy", None),
        P("gx", "gy", None),
        P("gx", "gy", None),
        P(),
        P(),
        P(),
    )
    out_specs = (P(None, "gx", "gy", None), P("gx", "gy", None))
    return jax.shard_map(
        per_device, mesh=mesh, in_specs=in_specs, out_specs=out_specs, check_vma=False
    )
```

profile of v0, /device:TPU:1, one launch (start us, length us, event | category | flops | bytes accessed | tf_op | source)
XLA Modules:
  0.0 361.1 jit_solution(15247358745443116115)
XLA Ops:
  3.5 4.2 %fusion.69 = (f32[1,16,16,512]{3,1,2,0:T(8,128)S(1)}, pred[16,16,512]{2,0,1:T(8,128)(4,1)S(1)}, pred[16,16,512]{2,0,1:T(8,128)(4,1)S(1)}, pred[16,16,512]{2,0,1:T(8,128)(4,1)S(1)}, pred[16,16,512]{2,0,1:T(8,128)(4,1)S(1)}) fusion(f32[]{:T(128)} %bitcast.8, f32[]{:T(128)} %bitcast.7, f32[]{:T(128)} %bitcast.6, f32[]{:T(128)} %bitcast.5, s32[16,16,512]{2,1,0:T(8,128)} %param.12), kind=kLoop, calls=%fused_computation.164 | loop fusion | flops 1441792 | bytes 1572880 | tf_op jit(solution)/shard_map/stack | solution.py:68
  7.7 3.5 fusion.65
  11.3 4.6 %collective-permute-start = (f32[2,1,16,512]{3,1,2,0:T(1,128)S(1)}, f32[2,1,16,512]{3,1,2,0:T(1,128)S(1)}, u32[]{:S(2)}, u32[]{:S(2)}) collective-permute-start(f32[2,1,16,512]{3,1,2,0:T(1,128)S(1)} %get-tuple-element.38), channel_id=1, source_target_pairs={{0,32},{32,64},{64,96},{96,128},{128,160},{160,192},{192,224},{1,3... | collective-permute-start | bytes 196616 | tf_op jit(solution)/shard_map/ppermute | solution.py:16
  15.9 1.9 collective-permute-start.1
  17.9 1.9 collective-permute-start.4
  19.8 3.6 %collective-permute-start.5 = (f32[3,1,16,512]{3,2,1,0:T(8,128)S(1)}, f32[3,1,16,512]{3,2,1,0:T(8,128)S(1)}, u32[]{:S(2)}, u32[]{:S(2)}) collective-permute-start(f32[3,1,16,512]{3,2,1,0:T(8,128)S(1)} %get-tuple-element.34), channel_id=1, source_target_pairs={{0,32},{32,64},{64,96},{96,128},{128,160},{160,192},{192,224},{1,3... | collective-permute-start | bytes 294920 | tf_op jit(solution)/shard_map/ppermute | solution.py:16
  25.5 3.1 collective-permute-start.2
  31.5 4.6 %collective-permute-start.7 = (f32[3,18,1,512]{3,1,2,0:T(8,128)S(1)}, f32[3,18,1,512]{3,1,2,0:T(8,128)S(1)}, u32[]{:S(2)}, u32[]{:S(2)}) collective-permute-start(f32[3,18,1,512]{3,1,2,0:T(8,128)S(1)} %get-tuple-element.28), channel_id=1, source_target_pairs={{0,1},{1,2},{2,3},{3,4},{4,5},{5,6},{6,7},{7,8},{8,9},{9,10},{10,1... | collective-permute-start | bytes 331784 | tf_op jit(solution)/shard_map/ppermute | solution.py:16
  39.6 3.2 select_maximum_fusion.8
  42.9 4.6 %multiply_reduce_fusion.1 = (f32[]{:T(128)}, f32[3,16,16,512]{3,1,2,0:T(8,128)S(1)}) fusion(f32[3,16,16,512]{3,2,1,0:T(8,128)S(1)} %copy-done, f32[3,18,18,514]{3,1,2,0:T(8,128)S(1)} %select_maximum_fusion.8, f32[16,16,512]{2,0,1:T(8,128)S(1)} %get-tuple-element.16, f32[16,16,512]{2,0,1:T(8,128)S(1)} %get-tuple-element.15, f32[3,1,16,512]{3,1,2,0:T(1,128)S(1)} %copy.37, ...), kind=kLoop, calls=%fused_computation.71 | loop fusion | flops 9043967 | bytes 11952132 | tf_op jit(solution)/shard_map/reduce_sum | solution.py:82
  47.5 84.1 %all-reduce.5 = (f32[]{:T(128)}, f32[]{:T(128)}) all-reduce(f32[]{:T(128)} %multiply_reduce_fusion.2, f32[]{:T(128)} %get-tuple-element.8), channel_id=1, replica_groups=mesh['gx'=8,'gy'=32] {'gx','gy'}, use_global_device_ids=true, to_apply=%region_1.2 | all-reduce | flops 2 | bytes 16 | tf_op jit(solution)/shard_map/psum | solution.py:46
  132.9 1.6 multiply_reduce_fusion
  134.6 74.5 %psum.30 = f32[]{:T(128)} all-reduce(f32[]{:T(128)} %multiply_reduce_fusion), channel_id=1, replica_groups=mesh['gx'=8,'gy'=32] {'gx','gy'}, use_global_device_ids=true, to_apply=%region_5.6 | all-reduce | flops 1 | bytes 8 | tf_op jit(solution)/shard_map/psum | solution.py:46
  210.3 2.5 multiply_add_fusion.1
  213.0 2.6 collective-permute-start.8
  215.6 3.0 collective-permute-start.9
  221.8 4.3 %collective-permute-start.11 = (f32[3,18,1,512]{3,1,2,0:T(8,128)S(1)}, f32[3,18,1,512]{3,1,2,0:T(8,128)S(1)}, u32[]{:S(2)}, u32[]{:S(2)}) collective-permute-start(f32[3,18,1,512]{3,1,2,0:T(8,128)S(1)} %get-tuple-element.26), channel_id=1, source_target_pairs={{0,1},{1,2},{2,3},{3,4},{4,5},{5,6},{6,7},{7,8},{8,9},{9,10},{10,1... | collective-permute-start | bytes 331784 | tf_op jit(solution)/shard_map/ppermute | solution.py:16
  227.1 2.1 collective-permute-done.11
  229.2 3.2 select_maximum_fusion.4
  232.5 3.3 fusion.4
  235.8 78.2 %psum.31 = f32[]{:T(128)} all-reduce(f32[]{:T(128)} %fusion.4), channel_id=1, replica_groups=mesh['gx'=8,'gy'=32] {'gx','gy'}, use_global_device_ids=true, to_apply=%region_7.8 | all-reduce | flops 1 | bytes 8 | tf_op jit(solution)/shard_map/psum | solution.py:82
  316.6 3.1 collective-permute-start.12
  319.8 2.4 collective-permute-start.13
  325.3 4.0 %collective-permute-start.15 = (f32[3,18,1,512]{3,1,2,0:T(8,128)S(1)}, f32[3,18,1,512]{3,1,2,0:T(8,128)S(1)}, u32[]{:S(2)}, u32[]{:S(2)}) collective-permute-start(f32[3,18,1,512]{3,1,2,0:T(8,128)S(1)} %get-tuple-element.24), channel_id=1, source_target_pairs={{0,1},{1,2},{2,3},{3,4},{4,5},{5,6},{6,7},{7,8},{8,9},{9,10},{10,1... | collective-permute-start | bytes 331784 | tf_op jit(solution)/shard_map/ppermute | solution.py:16
  331.3 1.6 collective-permute-done.15
  332.9 3.2 select_maximum_fusion
  336.2 3.5 fusion.50
  339.7 2.4 collective-permute-start.16
  342.0 3.5 collective-permute-start.17
  347.9 4.9 %collective-permute-start.19 = (f32[18,1,512]{2,0,1:T(8,128)S(1)}, f32[18,1,512]{2,0,1:T(8,128)S(1)}, u32[]{:S(2)}, u32[]{:S(2)}) collective-permute-start(f32[18,1,512]{2,0,1:T(8,128)S(1)} %get-tuple-element.40), channel_id=1, source_target_pairs={{0,1},{1,2},{2,3},{3,4},{4,5},{5,6},{6,7},{7,8},{8,9},{9,10},{10,1... | collective-permute-start | bytes 110600 | tf_op jit(solution)/shard_map/ppermute | solution.py:16
  352.8 2.1 copy.60
  356.1 3.9 %fusion.28 = f32[16,16,512]{2,0,1:T(8,128)S(1)} fusion(f32[16,16,512]{2,0,1:T(8,128)S(1)} %fusion.50, f32[18,18,514]{2,0,1:T(8,128)S(1)} %select_maximum_fusion.17, f32[18,18,514]{2,0,1:T(8,128)S(1)} %copy-done.3, f32[18,1,512]{2,0,1:T(8,128)S(1)} %collective-permute-done.19, f32[1,16,512]{2,0,1:T(1,128)S(1)} %collective-permute-done.16, ...), kind=kLoop, calls=%fused_computation.84 | loop fusion | flops 6029312 | bytes 5906448 | tf_op jit(solution)/shard_map/add | solution.py:97
  (104 shorter events, 26.5 us)
Async XLA Ops:
  0.6 7.1 %copy-start.22 = (s32[16,16,512]{2,1,0:T(8,128)S(1)}, s32[16,16,512]{2,1,0:T(8,128)}, u32[]{:S(2)}) copy-start(s32[16,16,512]{2,1,0:T(8,128)} %param.10) | copy-start | bytes 1572868
  7.7 10.1 %copy-start = (f32[3,16,16,512]{3,2,1,0:T(8,128)S(1)}, f32[3,16,16,512]{3,2,1,0:T(8,128)}, u32[]{:S(2)}) copy-start(f32[3,16,16,512]{3,2,1,0:T(8,128)} %param.8) | copy-start | bytes 4718596
  11.2 27.3 %copy-start.1 = (f32[16,16,512]{2,0,1:T(8,128)}, f32[16,16,512]{2,0,1:T(8,128)S(1)}, u32[]{:S(2)}) copy-start(f32[16,16,512]{2,0,1:T(8,128)S(1)} %fusion.65) | copy-start | bytes 1572868
  11.3 14.1 %collective-permute-start = (f32[2,1,16,512]{3,1,2,0:T(1,128)S(1)}, f32[2,1,16,512]{3,1,2,0:T(1,128)S(1)}, u32[]{:S(2)}, u32[]{:S(2)}) collective-permute-start(f32[2,1,16,512]{3,1,2,0:T(1,128)S(1)} %get-tuple-element.38), channel_id=1, source_target_pairs={{0,32},{32,64},{64,96},{96,128},{128,160},{160,192},{192,224},{1,3... | collective-permute-start | bytes 196616 | tf_op jit(solution)/shard_map/ppermute | solution.py:16
  15.9 9.5 %collective-permute-start.1 = (f32[2,1,16,512]{3,1,2,0:T(1,128)S(1)}, f32[2,1,16,512]{3,1,2,0:T(1,128)S(1)}, u32[]{:S(2)}, u32[]{:S(2)}) collective-permute-start(f32[2,1,16,512]{3,1,2,0:T(1,128)S(1)} %get-tuple-element.39), channel_id=1, source_target_pairs={{32,0},{64,32},{96,64},{128,96},{160,128},{192,160},{224,192},{33,... | collective-permute-start | bytes 196616 | tf_op jit(solution)/shard_map/ppermute | solution.py:17
  17.9 12.0 %collective-permute-start.4 = (f32[3,1,16,512]{3,2,1,0:T(8,128)S(1)}, f32[3,1,16,512]{3,2,1,0:T(8,128)S(1)}, u32[]{:S(2)}, u32[]{:S(2)}) collective-permute-start(f32[3,1,16,512]{3,2,1,0:T(8,128)S(1)} %get-tuple-element.35), channel_id=1, source_target_pairs={{32,0},{64,32},{96,64},{128,96},{160,128},{192,160},{224,192},{33,... | collective-permute-start | bytes 294920 | tf_op jit(solution)/shard_map/ppermute | solution.py:17
  19.8 10.2 %collective-permute-start.5 = (f32[3,1,16,512]{3,2,1,0:T(8,128)S(1)}, f32[3,1,16,512]{3,2,1,0:T(8,128)S(1)}, u32[]{:S(2)}, u32[]{:S(2)}) collective-permute-start(f32[3,1,16,512]{3,2,1,0:T(8,128)S(1)} %get-tuple-element.34), channel_id=1, source_target_pairs={{0,32},{32,64},{64,96},{96,128},{128,160},{160,192},{192,224},{1,3... | collective-permute-start | bytes 294920 | tf_op jit(solution)/shard_map/ppermute | solution.py:16
  25.5 10.7 %collective-permute-start.2 = (f32[2,18,1,512]{3,1,2,0:T(8,128)S(1)}, f32[2,18,1,512]{3,1,2,0:T(8,128)S(1)}, u32[]{:S(2)}, u32[]{:S(2)}) collective-permute-start(f32[2,18,1,512]{3,1,2,0:T(8,128)S(1)} %get-tuple-element.36), channel_id=1, source_target_pairs={{0,1},{1,2},{2,3},{3,4},{4,5},{5,6},{6,7},{7,8},{8,9},{9,10},{10,1... | collective-permute-start | bytes 221192 | tf_op jit(solution)/shard_map/ppermute | solution.py:16
  28.6 7.5 %collective-permute-start.3 = (f32[2,18,1,512]{3,1,2,0:T(8,128)S(1)}, f32[2,18,1,512]{3,1,2,0:T(8,128)S(1)}, u32[]{:S(2)}, u32[]{:S(2)}) collective-permute-start(f32[2,18,1,512]{3,1,2,0:T(8,128)S(1)} %get-tuple-element.37), channel_id=1, source_target_pairs={{1,0},{2,1},{3,2},{4,3},{5,4},{6,5},{7,6},{8,7},{9,8},{10,9},{11,1... | collective-permute-start | bytes 221192 | tf_op jit(solution)/shard_map/ppermute | solution.py:17
  30.2 9.1 %collective-permute-start.6 = (f32[3,18,1,512]{3,1,2,0:T(8,128)S(1)}, f32[3,18,1,512]{3,1,2,0:T(8,128)S(1)}, u32[]{:S(2)}, u32[]{:S(2)}) collective-permute-start(f32[3,18,1,512]{3,1,2,0:T(8,128)S(1)} %get-tuple-element.29), channel_id=1, source_target_pairs={{1,0},{2,1},{3,2},{4,3},{5,4},{6,5},{7,6},{8,7},{9,8},{10,9},{11,1... | collective-permute-start | bytes 331784 | tf_op jit(solution)/shard_map/ppermute | solution.py:17
  31.5 8.1 %collective-permute-start.7 = (f32[3,18,1,512]{3,1,2,0:T(8,128)S(1)}, f32[3,18,1,512]{3,1,2,0:T(8,128)S(1)}, u32[]{:S(2)}, u32[]{:S(2)}) collective-permute-start(f32[3,18,1,512]{3,1,2,0:T(8,128)S(1)} %get-tuple-element.28), channel_id=1, source_target_pairs={{0,1},{1,2},{2,3},{3,4},{4,5},{5,6},{6,7},{7,8},{8,9},{9,10},{10,1... | collective-permute-start | bytes 331784 | tf_op jit(solution)/shard_map/ppermute | solution.py:16
  47.5 87.0 %copy-start.4 = (f32[3,16,16,512]{3,1,2,0:T(8,128)}, f32[3,16,16,512]{3,1,2,0:T(8,128)S(1)}, u32[]{:S(2)}) copy-start(f32[3,16,16,512]{3,1,2,0:T(8,128)S(1)} %get-tuple-element.9) | copy-start | bytes 4718596
  213.0 5.9 %collective-permute-start.8 = (f32[3,1,16,512]{3,2,1,0:T(8,128)S(1)}, f32[3,1,16,512]{3,2,1,0:T(8,128)S(1)}, u32[]{:S(2)}, u32[]{:S(2)}) collective-permute-start(f32[3,1,16,512]{3,2,1,0:T(8,128)S(1)} %copy.47), channel_id=1, source_target_pairs={{32,0},{64,32},{96,64},{128,96},{160,128},{192,160},{224,192},{33,... | collective-permute-start | bytes 294920 | tf_op jit(solution)/shard_map/ppermute | solution.py:17
  215.6 4.6 %collective-permute-start.9 = (f32[3,1,16,512]{3,2,1,0:T(8,128)S(1)}, f32[3,1,16,512]{3,2,1,0:T(8,128)S(1)}, u32[]{:S(2)}, u32[]{:S(2)}) collective-permute-start(f32[3,1,16,512]{3,2,1,0:T(8,128)S(1)} %copy.49), channel_id=1, source_target_pairs={{0,32},{32,64},{64,96},{96,128},{128,160},{160,192},{192,224},{1,3... | collective-permute-start | bytes 294920 | tf_op jit(solution)/shard_map/ppermute | solution.py:16
  220.4 6.7 %collective-permute-start.10 = (f32[3,18,1,512]{3,1,2,0:T(8,128)S(1)}, f32[3,18,1,512]{3,1,2,0:T(8,128)S(1)}, u32[]{:S(2)}, u32[]{:S(2)}) collective-permute-start(f32[3,18,1,512]{3,1,2,0:T(8,128)S(1)} %get-tuple-element.27), channel_id=1, source_target_pairs={{1,0},{2,1},{3,2},{4,3},{5,4},{6,5},{7,6},{8,7},{9,8},{10,9},{11,1... | collective-permute-start | bytes 331784 | tf_op jit(solution)/shard_map/ppermute | solution.py:17
  221.7 10.7 %copy-start.6 = (f32[16,16,512]{2,0,1:T(8,128)S(1)}, f32[16,16,512]{2,0,1:T(8,128)}, u32[]{:S(2)}) copy-start(f32[16,16,512]{2,0,1:T(8,128)} %copy-done.5) | copy-start | bytes 1572868
  221.7 10.7 %copy-start.8 = (f32[16,16,512]{2,0,1:T(8,128)S(1)}, f32[16,16,512]{2,0,1:T(8,128)}, u32[]{:S(2)}) copy-start(f32[16,16,512]{2,0,1:T(8,128)} %copy-done.7) | copy-start | bytes 1572868
  221.7 10.7 %copy-start.10 = (f32[16,16,512]{2,0,1:T(8,128)S(1)}, f32[16,16,512]{2,0,1:T(8,128)}, u32[]{:S(2)}) copy-start(f32[16,16,512]{2,0,1:T(8,128)} %copy-done.9) | copy-start | bytes 1572868
  221.7 10.7 %copy-start.12 = (f32[16,16,512]{2,0,1:T(8,128)S(1)}, f32[16,16,512]{2,0,1:T(8,128)}, u32[]{:S(2)}) copy-start(f32[16,16,512]{2,0,1:T(8,128)} %copy-done.11) | copy-start | bytes 1572868
  221.8 10.7 %copy-start.14 = (f32[16,16,512]{2,0,1:T(8,128)S(1)}, f32[16,16,512]{2,0,1:T(8,128)}, u32[]{:S(2)}) copy-start(f32[16,16,512]{2,0,1:T(8,128)} %copy-done.13) | copy-start | bytes 1572868
  221.8 10.7 %copy-start.16 = (f32[16,16,512]{2,0,1:T(8,128)S(1)}, f32[16,16,512]{2,0,1:T(8,128)}, u32[]{:S(2)}) copy-start(f32[16,16,512]{2,0,1:T(8,128)} %copy-done.15) | copy-start | bytes 1572868
  221.8 10.7 %copy-start.18 = (f32[16,16,512]{2,0,1:T(8,128)S(1)}, f32[16,16,512]{2,0,1:T(8,128)}, u32[]{:S(2)}) copy-start(f32[16,16,512]{2,0,1:T(8,128)} %copy-done.17) | copy-start | bytes 1572868
  221.8 7.4 %collective-permute-start.11 = (f32[3,18,1,512]{3,1,2,0:T(8,128)S(1)}, f32[3,18,1,512]{3,1,2,0:T(8,128)S(1)}, u32[]{:S(2)}, u32[]{:S(2)}) collective-permute-start(f32[3,18,1,512]{3,1,2,0:T(8,128)S(1)} %get-tuple-element.26), channel_id=1, source_target_pairs={{0,1},{1,2},{2,3},{3,4},{4,5},{5,6},{6,7},{7,8},{8,9},{9,10},{10,1... | collective-permute-start | bytes 331784 | tf_op jit(solution)/shard_map/ppermute | solution.py:16
  316.4 12.9 %copy-start.24 = (f32[4]{0:T(128)S(1)}, f32[4]{0:T(128)}, u32[]{:S(2)}) copy-start(f32[4]{0:T(128)} %param.14) | copy-start | bytes 52
  316.6 5.9 %collective-permute-start.12 = (f32[3,1,16,512]{3,2,1,0:T(8,128)S(1)}, f32[3,1,16,512]{3,2,1,0:T(8,128)S(1)}, u32[]{:S(2)}, u32[]{:S(2)}) collective-permute-start(f32[3,1,16,512]{3,2,1,0:T(8,128)S(1)} %copy.54), channel_id=1, source_target_pairs={{32,0},{64,32},{96,64},{128,96},{160,128},{192,160},{224,192},{33,... | collective-permute-start | bytes 294920 | tf_op jit(solution)/shard_map/ppermute | solution.py:17
  319.8 4.0 %collective-permute-start.13 = (f32[3,1,16,512]{3,2,1,0:T(8,128)S(1)}, f32[3,1,16,512]{3,2,1,0:T(8,128)S(1)}, u32[]{:S(2)}, u32[]{:S(2)}) collective-permute-start(f32[3,1,16,512]{3,2,1,0:T(8,128)S(1)} %copy.56), channel_id=1, source_target_pairs={{0,32},{32,64},{64,96},{96,128},{128,160},{160,192},{192,224},{1,3... | collective-permute-start | bytes 294920 | tf_op jit(solution)/shard_map/ppermute | solution.py:16
  324.0 7.3 %collective-permute-start.14 = (f32[3,18,1,512]{3,1,2,0:T(8,128)S(1)}, f32[3,18,1,512]{3,1,2,0:T(8,128)S(1)}, u32[]{:S(2)}, u32[]{:S(2)}) collective-permute-start(f32[3,18,1,512]{3,1,2,0:T(8,128)S(1)} %get-tuple-element.25), channel_id=1, source_target_pairs={{1,0},{2,1},{3,2},{4,3},{5,4},{6,5},{7,6},{8,7},{9,8},{10,9},{11,1... | collective-permute-start | bytes 331784 | tf_op jit(solution)/shard_map/ppermute | solution.py:17
  325.3 7.6 %collective-permute-start.15 = (f32[3,18,1,512]{3,1,2,0:T(8,128)S(1)}, f32[3,18,1,512]{3,1,2,0:T(8,128)S(1)}, u32[]{:S(2)}, u32[]{:S(2)}) collective-permute-start(f32[3,18,1,512]{3,1,2,0:T(8,128)S(1)} %get-tuple-element.24), channel_id=1, source_target_pairs={{0,1},{1,2},{2,3},{3,4},{4,5},{5,6},{6,7},{7,8},{8,9},{9,10},{10,1... | collective-permute-start | bytes 331784 | tf_op jit(solution)/shard_map/ppermute | solution.py:16
  339.7 5.9 %collective-permute-start.16 = (f32[1,16,512]{2,0,1:T(1,128)S(1)}, f32[1,16,512]{2,0,1:T(1,128)S(1)}, u32[]{:S(2)}, u32[]{:S(2)}) collective-permute-start(f32[1,16,512]{2,0,1:T(1,128)S(1)} %get-tuple-element.43), channel_id=1, source_target_pairs={{32,0},{64,32},{96,64},{128,96},{160,128},{192,160},{224,192},{33,... | collective-permute-start | bytes 98312 | tf_op jit(solution)/shard_map/ppermute | solution.py:17
  342.0 4.5 %collective-permute-start.17 = (f32[1,16,512]{2,0,1:T(1,128)S(1)}, f32[1,16,512]{2,0,1:T(1,128)S(1)}, u32[]{:S(2)}, u32[]{:S(2)}) collective-permute-start(f32[1,16,512]{2,0,1:T(1,128)S(1)} %get-tuple-element.42), channel_id=1, source_target_pairs={{0,32},{32,64},{64,96},{96,128},{128,160},{160,192},{192,224},{1,3... | collective-permute-start | bytes 98312 | tf_op jit(solution)/shard_map/ppermute | solution.py:16
  346.6 8.3 %collective-permute-start.18 = (f32[18,1,512]{2,0,1:T(8,128)S(1)}, f32[18,1,512]{2,0,1:T(8,128)S(1)}, u32[]{:S(2)}, u32[]{:S(2)}) collective-permute-start(f32[18,1,512]{2,0,1:T(8,128)S(1)} %get-tuple-element.41), channel_id=1, source_target_pairs={{1,0},{2,1},{3,2},{4,3},{5,4},{6,5},{7,6},{8,7},{9,8},{10,9},{11,1... | collective-permute-start | bytes 110600 | tf_op jit(solution)/shard_map/ppermute | solution.py:17
  347.9 7.0 %collective-permute-start.19 = (f32[18,1,512]{2,0,1:T(8,128)S(1)}, f32[18,1,512]{2,0,1:T(8,128)S(1)}, u32[]{:S(2)}, u32[]{:S(2)}) collective-permute-start(f32[18,1,512]{2,0,1:T(8,128)S(1)} %get-tuple-element.40), channel_id=1, source_target_pairs={{0,1},{1,2},{2,3},{3,4},{4,5},{5,6},{6,7},{7,8},{8,9},{9,10},{10,1... | collective-permute-start | bytes 110600 | tf_op jit(solution)/shard_map/ppermute | solution.py:16
  (13 other events, 55.5 us)
where the time goes:
time: 368 us; the launch traced here: 361 us
  blocking collectives  237 us (64%)
  starting transfers between devices  56.4 us (15%)
  other arithmetic  41.6 us (11%)
  local copies, waits for them, and re-layouts  10.6 us (3%)
  waiting for transfers between devices  10.4 us (3%)
  between operations  5.25 us (1%)
    psum x2, blocking collectives, squares(): return lax.psum(jnp.sum(residual * residual), ('gx', 'gy'))  159 us
    psum x1, blocking collectives, per_device(): step_size = norm_now / lax.psum(jnp.sum(direction * total), ('gx', 'gy'))  78.2 us
    ppermute x10, starting transfers between devices, with_halo(): before = lax.ppermute(last, axis, up)  38.1 us
    ppermute x10, starting transfers between devices, with_halo(): after = lax.ppermute(leading, axis, down)  18.4 us
    concatenate x9, other arithmetic, with_halo(): array = jnp.concatenate([before, array, after], axis=dim)  11.5 us
    reduce_sum x2, other arithmetic, per_device(): step_size = norm_now / lax.psum(jnp.sum(direction * total), ('gx', 'gy'))  7.97 us
  transfers between devices with their start and end apart: 20, of which 10 were waited for; matrix products, arithmetic and copies ran while one was open for 2% of the time, Pallas kernels for 0%

commit v1 on v0

v1 whole, which is shorter than its diff:
```python
import functools

import jax
import jax.numpy as jnp
from jax import lax
from jax.experimental import pallas as pl
from jax.experimental.pallas import tpu as pltpu
from jax.sharding import PartitionSpec as P

MESH = pl.DeviceIdType.MESH
RING_X = 4


def pick(table, label):
    low = jnp.where(label == 0, table[0], table[1])
    high = jnp.where(label == 2, table[2], table[3])
    return jnp.where(label < 2, low, high)


def fold(plane):
    rows, lanes = plane.shape
    total = None
    for i in range(0, rows, 8):
        for j in range(0, lanes, 128):
            part = plane[i : i + 8, j : j + 128]
            total = part if total is None else total + part
    return total


def kernel(
    gx_size, gy_size,
    b_hbm, warm_hbm, yield_hbm, print_hbm, label_hbm, rigidity, dilatation, diffusivity,
    x_out, th_out,
    B, U, H, WARM, YIELD, PRINT, LABEL, TS, WY, WZ, D, S3, T,
    y1_lo, y1_hi, r1_lo, r1_hi,
    y2_lo, y2_hi, r2_lo, r2_hi,
    y3_lo, y3_hi, r3_lo, r3_hi,
    sums,
    load_sem, send1, recv1, send2, recv2, send3, recv3, send_r, recv_r,
):
    _, nx, ny, nz = b_hbm.shape
    gx, gy = lax.axis_index("gx"), lax.axis_index("gy")
    ring_z = gy_size // RING_X
    gz, gq = gy // RING_X, gy % RING_X
    up_x, down_x = (gx + 1) % gx_size, (gx + gx_size - 1) % gx_size
    up_y, down_y = (gy + 1) % gy_size, (gy + gy_size - 1) % gy_size
    stages = []
    for stage, count in enumerate((gx_size, ring_z, RING_X)):
        partners = []
        for k in range(1, count):
            if stage == 0:
                partners.append(((gx + k) % gx_size, gy))
            elif stage == 1:
                partners.append((gx, ((gz + k) % ring_z) * RING_X + gq))
            else:
                partners.append((gx, gz * RING_X + (gq + k) % RING_X))
        stages.append(partners)

    loads = [
        pltpu.make_async_copy(label_hbm, LABEL, load_sem.at[0]),
        pltpu.make_async_copy(yield_hbm, YIELD, load_sem.at[1]),
        pltpu.make_async_copy(print_hbm, PRINT, load_sem.at[2]),
        pltpu.make_async_copy(warm_hbm, WARM, load_sem.at[3]),
        pltpu.make_async_copy(b_hbm, B.at[:, pl.ds(1, nx)], load_sem.at[4]),
    ]
    for load in loads:
        load.start()

    barrier = pltpu.get_barrier_semaphore()
    greeted = [(up_x, gy), (down_x, gy), (gx, up_y), (gx, down_y)]
    for partners in stages:
        greeted += partners
    for partner in greeted:
        pl.semaphore_signal(barrier, inc=1, device_id=partner, device_id_type=MESH)

    row = lax.broadcasted_iota(jnp.int32, (ny, nz), 0)
    lane = lax.broadcasted_iota(jnp.int32, (ny, nz), 1)
    first_row, last_row = row == 0, row == ny - 1
    last_lane = lane == nz - 1
    edge_lane = (lane == 0) | last_lane

    def remote(src, dst, send, recv, partner):
        return pltpu.make_async_remote_copy(
            src_ref=src, dst_ref=dst, send_sem=send, recv_sem=recv,
            device_id=partner, device_id_type=MESH,
        )

    def faces(field, ylo, yhi, rlo, rhi, send, recv, base):
        lead = (slice(None),) * (len(field.shape) - 3)
        at = lambda i: field.at[lead + (i,)]
        return [
            remote(at(nx), at(0), send.at[base], recv.at[base], (up_x, gy)),
            remote(at(1), at(nx + 1), send.at[base + 1], recv.at[base + 1], (down_x, gy)),
            remote(yhi, rlo, send.at[base + 2], recv.at[base + 2], (gx, up_y)),
            remote(ylo, rhi, send.at[base + 3], recv.at[base + 3], (gx, down_y)),
        ]

    for load in loads:
        load.wait()

    def properties(x, carry):
        label = LABEL[x]
        stiffness = (
            pick(rigidity, label)
            * (1.0 - 0.7 * YIELD[x].astype(jnp.float32))
            * (0.05 + 0.95 * PRINT[x].astype(jnp.float32))
        )
        half = 0.5 * stiffness
        H[x + 1] = half
        TS[x] = pick(dilatation, label) * (0.5 + WARM[x]) * half
        half_c = 0.5 * pick(diffusivity, label)
        S3[2, x + 1] = half_c
        at = pl.ds(x, 1)
        for c in range(3):
            y1_lo[c, at, :] = B[c, x + 1, 0:1, :]
            y1_hi[c, at, :] = B[c, x + 1, ny - 1 : ny, :]
        y1_lo[3, at, :] = half[0:1, :]
        y1_hi[3, at, :] = half[ny - 1 : ny, :]
        y3_lo[2, at, :] = half_c[0:1, :]
        y3_hi[2, at, :] = half_c[ny - 1 : ny, :]
        return carry

    lax.fori_loop(0, nx, properties, 0)

    pl.semaphore_wait(barrier, len(greeted))

    copies1 = faces(B, y1_lo, y1_hi, r1_lo, r1_hi, send1, recv1, 0)
    copies1 += [
        remote(H.at[nx], H.at[0], send1.at[4], recv1.at[4], (up_x, gy)),
        remote(H.at[1], H.at[nx + 1], send1.at[5], recv1.at[5], (down_x, gy)),
    ]
    for copy in copies1:
        copy.start()
    for copy in copies1:
        copy.wait()

    def clear(field, rlo, rhi):
        lead = (slice(None),) * (len(field.shape) - 3)

        @pl.when(gx == 0)
        def _():
            field[lead + (0,)] = jnp.zeros(field.shape[:-3] + (ny, nz), jnp.float32)

        @pl.when(gx == gx_size - 1)
        def _():
            field[lead + (nx + 1,)] = jnp.zeros(field.shape[:-3] + (ny, nz), jnp.float32)

        if rlo is None:
            return

        @pl.when(gy == 0)
        def _():
            rlo[...] = jnp.zeros(rlo.shape, jnp.float32)

        @pl.when(gy == gy_size - 1)
        def _():
            rhi[...] = jnp.zeros(rhi.shape, jnp.float32)

    clear(B, r1_lo, r1_hi)
    clear(H, None, None)

    def next_y(plane, row_hi):
        return jnp.where(last_row, row_hi, pltpu.roll(plane, ny - 1, 0))

    def prev_y(plane, row_lo):
        return jnp.where(first_row, row_lo, pltpu.roll(plane, 1, 0))

    def next_z(plane):
        return pltpu.roll(plane, nz - 1, 1)

    def prev_z(plane):
        return pltpu.roll(plane, 1, 1)

    def inflow(here, below, above, row_lo, row_hi, wxm, wxp, wy, wz, wlo):
        total = wxp * (above - here) + wxm * (below - here)
        flux = wy * (next_y(here, row_hi) - here)
        total += flux - prev_y(flux, wlo * (here[0:1, :] - row_lo))
        flux = wz * (next_z(here) - here)
        return total + (flux - prev_z(flux))

    zero = jnp.zeros((8, 128), jnp.float32)

    def first_image(x, carry):
        bu, uu = carry
        at = pl.ds(x, 1)
        half = H[x + 1]
        wxp, wxm = half + H[x + 2], half + H[x]
        wlo = half[0:1, :] + r1_lo[3, at, :]
        wy = half + next_y(half, r1_hi[3, at, :])
        wz = jnp.where(last_lane, 0.0, half + next_z(half))
        diag = 0.5 + jnp.where(edge_lane, half, 0.0)
        WY[x], WZ[x], D[x] = wy, wz, diag
        for c in range(3):
            here = B[c, x + 1]
            image = diag * here - inflow(
                here, B[c, x], B[c, x + 2], r1_lo[c, at, :], r1_hi[c, at, :],
                wxm, wxp, wy, wz, wlo,
            )
            U[c, x + 1] = image
            y2_lo[c, at, :] = image[0:1, :]
            y2_hi[c, at, :] = image[ny - 1 : ny, :]
            bu += fold(here * image)
            uu += fold(image * image)
        return bu, uu

    bu, uu = lax.fori_loop(0, nx, first_image, (zero, zero))

    copies2 = faces(U, y2_lo, y2_hi, r2_lo, r2_hi, send2, recv2, 0)
    for copy in copies2:
        copy.start()

    def everywhere(tile):
        total = jnp.sum(jnp.sum(tile, axis=0, keepdims=True), axis=1, keepdims=True)
        return jnp.broadcast_to(total, (1, 128))

    weight = everywhere(uu)
    sigma = everywhere(bu) / jnp.where(weight > 0.0, weight, 1.0)

    def source_of(field, rlo, rhi, out, ylo, yhi):
        def body(x, carry):
            at = pl.ds(x, 1)
            mid, last = field[1, x + 1], field[2, x + 1]
            div = field[0, x + 2] - field[0, x]
            div += next_y(mid, rhi[1, at, :]) - prev_y(mid, rlo[1, at, :])
            div += jnp.where(last_lane, 0.0, next_z(last)) - jnp.where(lane == 0, 0.0, prev_z(last))
            source = -TS[x] * div
            S3[out, x + 1] = source
            ylo[out, at, :] = source[0:1, :]
            yhi[out, at, :] = source[ny - 1 : ny, :]
            return carry

        lax.fori_loop(0, nx, body, 0)

    source_of(B, r1_lo, r1_hi, 0, y3_lo, y3_hi)

    for copy in copies2:
        copy.wait()
    clear(U, r2_lo, r2_hi)

    sigma_all = jnp.broadcast_to(sigma[:, 0:1], (ny, nz))

    def second_image(x, carry):
        rr, ru, rv, uv = carry
        at = pl.ds(x, 1)
        half = H[x + 1]
        wxp, wxm = half + H[x + 2], half + H[x]
        wlo = half[0:1, :] + r1_lo[3, at, :]
        wy, wz, diag = WY[x], WZ[x], D[x]
        for c in range(3):
            here = U[c, x + 1]
            image = diag * here - inflow(
                here, U[c, x], U[c, x + 2], r2_lo[c, at, :], r2_hi[c, at, :],
                wxm, wxp, wy, wz, wlo,
            )
            rest = B[c, x + 1] - sigma_all * here
            rr += fold(rest * rest)
            ru += fold(rest * here)
            rv += fold(rest * image)
            uv += fold(here * image)
        return rr, ru, rv, uv

    moments = lax.fori_loop(0, nx, second_image, (zero,) * 4)

    def lanes(tile):
        return jnp.sum(tile, axis=0, keepdims=True)

    def pack(parts):
        index = lax.broadcasted_iota(jnp.int32, (8, 128), 0)
        tile = jnp.zeros((8, 128), jnp.float32)
        for i, part in enumerate(parts):
            tile = jnp.where(index == i, jnp.broadcast_to(part, (8, 128)), tile)
        return tile

    def merge(tiles):
        rows = [[tile[i : i + 1, :] for i in range(7)] for tile in tiles]
        weight = sum(r[6] for r in rows)
        sigma = sum(r[6] * r[5] for r in rows) / jnp.where(weight > 0.0, weight, 1.0)
        out = [0.0] * 5
        for uu, rr, ru, rv, uv, own, _ in rows:
            tau = own - sigma
            shifted = (
                uu, rr + tau * (2.0 * ru + tau * uu), ru + tau * uu, rv + tau * uv, uv,
            )
            out = [a + b for a, b in zip(out, shifted)]
        return out + [sigma, weight]

    state = [lanes(uu)] + [lanes(m) for m in moments] + [sigma, weight]

    def reduce_start(stage, state):
        base = sum(len(s) for s in stages[:stage])
        own = sums.at[base + stage]
        sums[base + stage] = pack(state)
        copies = []
        for k, partner in enumerate(stages[stage]):
            copies.append(
                remote(own, sums.at[base + stage + 1 + k], send_r.at[base + k], recv_r.at[base + k], partner)
            )
        for copy in copies:
            copy.start()
        return copies

    def reduce_finish(stage, copies):
        base = sum(len(s) for s in stages[:stage]) + stage
        for copy in copies:
            copy.wait()
        return merge([sums[base + k] for k in range(len(copies) + 1)])

    pending = reduce_start(0, state)
    source_of(U, r2_lo, r2_hi, 1, y3_lo, y3_hi)
    copies3 = faces(S3, y3_lo, y3_hi, r3_lo, r3_hi, send3, recv3, 0)
    for copy in copies3:
        copy.start()
    state = reduce_finish(0, pending)
    pending = reduce_start(1, state)
    for copy in copies3:
        copy.wait()
    clear(S3, r3_lo, r3_hi)
    state = reduce_finish(1, pending)
    pending = reduce_start(2, state)

    def conduct(x, carry):
        at = pl.ds(x, 1)
        half = S3[2, x + 1]
        wxp, wxm = half + S3[2, x + 2], half + S3[2, x]
        wlo = half[0:1, :] + r3_lo[2, at, :]
        wy = half + next_y(half, r3_hi[2, at, :])
        wz = jnp.where(last_lane, 0.0, half + next_z(half))
        diag = 1.0 - 0.15 * jnp.where(edge_lane, half, 0.0)
        for c in range(2):
            here = S3[c, x + 1]
            T[c, x] = diag * here + 0.15 * inflow(
                here, S3[c, x], S3[c, x + 2], r3_lo[c, at, :], r3_hi[c, at, :],
                wxm, wxp, wy, wz, wlo,
            )
        return carry

    lax.fori_loop(0, nx, conduct, 0)
    state = reduce_finish(2, pending)

    uu, rr, ru, rv, uv, sigma = [
        jnp.sum(part, axis=1, keepdims=True) for part in state[:5]
    ] + [state[5][:, 0:1]]
    energy = ru + sigma * uu
    norm = rr + sigma * (2.0 * ru + sigma * uu)
    step0 = norm / energy
    tau = sigma - step0
    norm1 = rr + tau * (2.0 * ru + tau * uu)
    ru, rv = ru + tau * uu, rv + tau * uv
    ratio = norm1 / norm
    curve = (ru - step0 * rv) + ratio * (2.0 * ru + ratio * energy)
    step1 = norm1 / curve
    coef_b = jnp.broadcast_to(step0 + step1 * (1.0 + ratio), (ny, nz))
    coef_u = jnp.broadcast_to(-step1 * step0, (ny, nz))

    def combine(x, carry):
        for c in range(3):
            x_out[c, x] = coef_b * B[c, x + 1] + coef_u * U[c, x + 1]
        th_out[x] = coef_b * T[0, x] + coef_u * T[1, x]
        return carry

    lax.fori_loop(0, nx, combine, 0)


def per_device(*args):
    b = args[0]
    _, nx, ny, nz = b.shape
    gx_size, gy_size = lax.axis_size("gx"), lax.axis_size("gy")
    partners = gx_size - 1 + gy_size // RING_X - 1 + RING_X - 1
    f32 = jnp.float32
    plane = (ny, nz)
    face = (nx, nz)
    hbm, smem, vmem = (
        pl.BlockSpec(memory_space=m) for m in (pl.ANY, pltpu.SMEM, pltpu.VMEM)
    )
    dma = pltpu.SemaphoreType.DMA
    scratch = [
        pltpu.VMEM((3, nx + 2) + plane, f32),
        pltpu.VMEM((3, nx + 2) + plane, f32),
        pltpu.VMEM((nx + 2,) + plane, f32),
        pltpu.VMEM((nx,) + plane, f32),
        pltpu.VMEM((nx,) + plane, jnp.int32),
        pltpu.VMEM((nx,) + plane, jnp.int32),
        pltpu.VMEM((nx,) + plane, jnp.int32),
        pltpu.VMEM((nx,) + plane, f32),
        pltpu.VMEM((nx,) + plane, f32),
        pltpu.VMEM((nx,) + plane, f32),
        pltpu.VMEM((nx,) + plane, f32),
        pltpu.VMEM((3, nx + 2) + plane, f32),
        pltpu.VMEM((2, nx) + plane, f32),
    ]
    for fields in (4, 3, 3):
        scratch += [pltpu.VMEM((fields,) + face, f32)] * 4
    scratch += [
        pltpu.VMEM((partners + 3, 8, 128), f32),
        dma((5,)), dma((6,)), dma((6,)), dma((4,)), dma((4,)), dma((4,)), dma((4,)),
        dma((partners,)), dma((partners,)),
    ]
    return pl.pallas_call(
        functools.partial(kernel, gx_size, gy_size),
        out_shape=(
            jax.ShapeDtypeStruct(b.shape, f32),
            jax.ShapeDtypeStruct(b.shape[1:], f32),
        ),
        in_specs=[hbm] * 5 + [smem] * 3,
        out_specs=(vmem, vmem),
        scratch_shapes=scratch,
        compiler_params=pltpu.CompilerParams(
            collective_id=0, has_side_effects=True, vmem_limit_bytes=48 * 1024 * 1024
        ),
        name="adjoint",
    )(*args)


def solution(mesh):
    in_specs = (
        P(None, "gx", "gy", None),
        P("gx", "gy", None),
        P("gx", "gy", None),
        P("gx", "gy", None),
        P("gx", "gy", None),
        P(),
        P(),
        P(),
    )
    out_specs = (P(None, "gx", "gy", None), P("gx", "gy", None))
    return jax.shard_map(
        per_device, mesh=mesh, in_specs=in_specs, out_specs=out_specs, check_vma=False
    )
```

time: 368 us -> 50 us (0.14); the launches traced: 361 us -> 49.7 us
  blocking collectives: 237 us -> 0 us
  starting transfers between devices: 56.4 us -> 0 us
  other arithmetic: 41.6 us -> 0 us
  Pallas kernels: 0 us -> 39.6 us
  waiting for transfers between devices: 10.4 us -> 0 us
  between operations: 5.25 us -> 0.66 us
    psum x3 -> x0, blocking collectives: 237 us -> none  [the longest x2 159 us: squares(): return lax.psum(jnp.sum(residual * residual), ('gx', 'gy'))]
    ppermute x20 -> x0, starting transfers between devices: 56.4 us -> none  [the longest x10 38.1 us: with_halo(): before = lax.ppermute(last, axis, up)]
    pallas_call x0 -> x1, Pallas kernels: none -> 39.6 us  [per_device(): pl.pallas_call(functools.partial(kernel, gx_size, gy_size), out_shape=(ja...]
    concatenate x9 -> x0, other arithmetic: 11.5 us -> none  [with_halo(): array = jnp.concatenate([before, array, after], axis=dim)]
    reduce_sum x4 -> x0, other arithmetic: 10.6 us -> none  [the longest x2 7.97 us: per_device(): step_size = norm_now / lax.psum(jnp.sum(direction * total), ('gx', 'gy'))]
    ppermute x20 -> x0, waiting for transfers between devices: 10.4 us -> none  [the longest x10 7.31 us: with_halo(): before = lax.ppermute(last, axis, up)]
    add x4 -> x0, other arithmetic: 8.26 us -> none  [the longest x1 3.91 us: per_device(): thermal = energy_input + 0.15 * change]
    mul x2 -> x0, other arithmetic: 6.91 us -> none  [the longest x1 3.45 us: per_device(): energy_input = -0.5 * thermal_scaling * flux_balance]
  transfers between devices with their start and end apart: 20 -> 0, of which waited for: 10 -> 0; matrix products, arithmetic and copies ran while one was open for 2% -> 0% of each run, Pallas kernels for 0% -> 0%
where the time goes in v1:
time: 50 us; the launch traced here: 49.7 us
  Pallas kernels  39.6 us (79%)
  local copies, waits for them, and re-layouts  9.47 us (19%)
  between operations  0.66 us (1%)
    pallas_call x1, Pallas kernels, per_device(): pl.pallas_call(functools.partial(kernel, gx_size, gy_size), out_shape=(ja...  39.6 us
    unnamed x18, local copies, waits for them, and re-layouts  9.47 us

profile of v1, /device:TPU:1, one launch (start us, length us, event | category | flops | bytes accessed | tf_op | source)
XLA Modules:
  0.0 49.7 jit_solution(1224895584381291242)
XLA Ops:
  0.6 0.0 copy-start
  0.6 1.4 %copy-done = f32[3,16,16,512]{3,2,1,0:T(8,128)S(1)} copy-done((f32[3,16,16,512]{3,2,1,0:T(8,128)S(1)}, f32[3,16,16,512]{3,2,1,0:T(8,128)}, u32[]{:S(2)}) %copy-start) | copy-done | bytes 1572888
  2.0 0.0 copy-start.1
  2.0 1.0 %copy-done.1 = f32[16,16,512]{2,1,0:T(8,128)S(1)} copy-done((f32[16,16,512]{2,1,0:T(8,128)S(1)}, f32[16,16,512]{2,1,0:T(8,128)}, u32[]{:S(2)}) %copy-start.1) | copy-done | bytes 524312
  3.1 0.0 copy-start.2
  3.1 1.0 %copy-done.2 = s32[16,16,512]{2,1,0:T(8,128)S(1)} copy-done((s32[16,16,512]{2,1,0:T(8,128)S(1)}, s32[16,16,512]{2,1,0:T(8,128)}, u32[]{:S(2)}) %copy-start.2) | copy-done | bytes 524312
  4.1 0.0 copy-start.3
  4.1 1.0 %copy-done.3 = s32[16,16,512]{2,1,0:T(8,128)S(1)} copy-done((s32[16,16,512]{2,1,0:T(8,128)S(1)}, s32[16,16,512]{2,1,0:T(8,128)}, u32[]{:S(2)}) %copy-start.3) | copy-done | bytes 524312
  5.2 0.0 copy-start.4
  5.2 1.0 %copy-done.4 = s32[16,16,512]{2,1,0:T(8,128)S(1)} copy-done((s32[16,16,512]{2,1,0:T(8,128)S(1)}, s32[16,16,512]{2,1,0:T(8,128)}, u32[]{:S(2)}) %copy-start.4) | copy-done | bytes 524312
  6.2 0.0 copy-start.5
  6.2 0.7 %copy-done.5 = f32[4]{0:T(128)S(1)} copy-done((f32[4]{0:T(128)S(1)}, f32[4]{0:T(128)}, u32[]{:S(2)}) %copy-start.5) | copy-done | bytes 40
  6.9 0.0 copy-start.6
  6.9 0.7 %copy-done.6 = f32[4]{0:T(128)S(1)} copy-done((f32[4]{0:T(128)S(1)}, f32[4]{0:T(128)}, u32[]{:S(2)}) %copy-start.6) | copy-done | bytes 40
  7.5 0.0 copy-start.7
  7.5 0.7 %copy-done.7 = f32[4]{0:T(128)S(1)} copy-done((f32[4]{0:T(128)S(1)}, f32[4]{0:T(128)}, u32[]{:S(2)}) %copy-start.7) | copy-done | bytes 40
  8.2 39.6 %adjoint.1 = (f32[3,16,16,512]{3,2,1,0:T(8,128)S(1)}, f32[16,16,512]{2,1,0:T(8,128)S(1)}) custom-call(f32[3,16,16,512]{3,2,1,0:T(8,128)S(1)} %copy-done, f32[16,16,512]{2,1,0:T(8,128)S(1)} %copy-done.1, s32[16,16,512]{2,1,0:T(8,128)S(1)} %copy-done.2, s32[16,16,512]{2,1,0:T(8,128)S(1)} %copy-done.3, s32[16,16,512]{2,1,0:T(8,128)S(1)} %copy-done.4, ...), custom_call_target="tpu_custom_call" | custom-call | tf_op jit(solution)/shard_map/adjoint/pallas_call | solution.py:398
  47.7 1.1 %copy.12 = f32[3,16,16,512]{3,2,1,0:T(8,128)} copy(f32[3,16,16,512]{3,2,1,0:T(8,128)S(1)} %get-tuple-element.4) | data formatting | bytes 3145728
  48.9 0.8 %copy.13 = f32[16,16,512]{2,1,0:T(8,128)} copy(f32[16,16,512]{2,1,0:T(8,128)S(1)} %get-tuple-element.5) | data formatting | bytes 1048576
Async XLA Ops:
  0.6 1.4 %copy-start = (f32[3,16,16,512]{3,2,1,0:T(8,128)S(1)}, f32[3,16,16,512]{3,2,1,0:T(8,128)}, u32[]{:S(2)}) copy-start(f32[3,16,16,512]{3,2,1,0:T(8,128)} %b_hbm.1) | copy-start | bytes 4718596
  2.0 1.0 %copy-start.1 = (f32[16,16,512]{2,1,0:T(8,128)S(1)}, f32[16,16,512]{2,1,0:T(8,128)}, u32[]{:S(2)}) copy-start(f32[16,16,512]{2,1,0:T(8,128)} %warm_hbm.1) | copy-start | bytes 1572868
  3.1 1.0 %copy-start.2 = (s32[16,16,512]{2,1,0:T(8,128)S(1)}, s32[16,16,512]{2,1,0:T(8,128)}, u32[]{:S(2)}) copy-start(s32[16,16,512]{2,1,0:T(8,128)} %yield_hbm.1) | copy-start | bytes 1572868
  4.1 1.0 %copy-start.3 = (s32[16,16,512]{2,1,0:T(8,128)S(1)}, s32[16,16,512]{2,1,0:T(8,128)}, u32[]{:S(2)}) copy-start(s32[16,16,512]{2,1,0:T(8,128)} %print_hbm.1) | copy-start | bytes 1572868
  5.2 1.0 %copy-start.4 = (s32[16,16,512]{2,1,0:T(8,128)S(1)}, s32[16,16,512]{2,1,0:T(8,128)}, u32[]{:S(2)}) copy-start(s32[16,16,512]{2,1,0:T(8,128)} %label_hbm.1) | copy-start | bytes 1572868
  6.2 0.7 %copy-start.5 = (f32[4]{0:T(128)S(1)}, f32[4]{0:T(128)}, u32[]{:S(2)}) copy-start(f32[4]{0:T(128)} %rigidity.1) | copy-start | bytes 52
  6.9 0.7 %copy-start.6 = (f32[4]{0:T(128)S(1)}, f32[4]{0:T(128)}, u32[]{:S(2)}) copy-start(f32[4]{0:T(128)} %dilatation.1) | copy-start | bytes 52
  7.5 0.7 %copy-start.7 = (f32[4]{0:T(128)S(1)}, f32[4]{0:T(128)}, u32[]{:S(2)}) copy-start(f32[4]{0:T(128)} %diffusivity.1) | copy-start | bytes 52

commit v2 on v1

v2 whole, which is shorter than its diff:
```python
import functools

import jax
import jax.numpy as jnp
from jax import lax
from jax.experimental import pallas as pl
from jax.experimental.pallas import tpu as pltpu
from jax.sharding import PartitionSpec as P

MESH = pl.DeviceIdType.MESH
RING_X = 4


def pick(table, label):
    low = jnp.where(label == 0, table[0], table[1])
    high = jnp.where(label == 2, table[2], table[3])
    return jnp.where(label < 2, low, high)


def fold(plane):
    rows, lanes = plane.shape
    total = None
    for i in range(0, rows, 8):
        for j in range(0, lanes, 128):
            part = plane[i : i + 8, j : j + 128]
            total = part if total is None else total + part
    return total


def kernel(
    gx_size, gy_size,
    b_hbm, warm_hbm, yield_hbm, print_hbm, label_hbm, rigidity_hbm, dilatation_hbm, diffusivity_hbm,
    U, T, coef_out,
    B, H, WARM, YIELD, PRINT, LABEL, TS, WY, WZ, D, S3,
    y1_lo, y1_hi, ry1_lo, ry1_hi, rx1_lo, rx1_hi,
    y2_lo, y2_hi, ry2_lo, ry2_hi, rx2_lo, rx2_hi,
    y3_lo, y3_hi, ry3_lo, ry3_hi, rx3_lo, rx3_hi,
    sums,
    rigidity, dilatation, diffusivity,
    load_sem, send1, recv1, send2, recv2, send3, recv3, send_r, recv_r,
):
    _, nx, ny, nz = b_hbm.shape
    gx, gy = lax.axis_index("gx"), lax.axis_index("gy")
    ring_z = gy_size // RING_X
    gz, gq = gy // RING_X, gy % RING_X
    up_x, down_x = (gx + 1) % gx_size, (gx + gx_size - 1) % gx_size
    up_y, down_y = (gy + 1) % gy_size, (gy + gy_size - 1) % gy_size
    has_lo_x, has_hi_x = gx > 0, gx < gx_size - 1
    has_lo_y, has_hi_y = gy > 0, gy < gy_size - 1
    stages = []
    for stage, count in enumerate((gx_size, ring_z, RING_X)):
        partners = []
        for k in range(1, count):
            if stage == 0:
                partners.append(((gx + k) % gx_size, gy))
            elif stage == 1:
                partners.append((gx, ((gz + k) % ring_z) * RING_X + gq))
            else:
                partners.append((gx, gz * RING_X + (gq + k) % RING_X))
        stages.append(partners)

    loads = [
        pltpu.make_async_copy(rigidity_hbm, rigidity, load_sem.at[5]),
        pltpu.make_async_copy(dilatation_hbm, dilatation, load_sem.at[6]),
        pltpu.make_async_copy(diffusivity_hbm, diffusivity, load_sem.at[7]),
        pltpu.make_async_copy(label_hbm, LABEL, load_sem.at[0]),
        pltpu.make_async_copy(yield_hbm, YIELD, load_sem.at[1]),
        pltpu.make_async_copy(print_hbm, PRINT, load_sem.at[2]),
        pltpu.make_async_copy(warm_hbm, WARM, load_sem.at[3]),
        pltpu.make_async_copy(b_hbm, B, load_sem.at[4]),
    ]
    for load in loads:
        load.start()

    barrier = pltpu.get_barrier_semaphore()
    greeted = [(up_x, gy), (down_x, gy), (gx, up_y), (gx, down_y)]
    for partners in stages:
        greeted += partners
    for partner in greeted:
        pl.semaphore_signal(barrier, inc=1, device_id=partner, device_id_type=MESH)

    for inside, halos in (
        (has_lo_x, (rx1_lo, rx2_lo, rx3_lo)),
        (has_hi_x, (rx1_hi, rx2_hi, rx3_hi)),
        (has_lo_y, (ry1_lo, ry2_lo, ry3_lo)),
        (has_hi_y, (ry1_hi, ry2_hi, ry3_hi)),
    ):
        @pl.when(jnp.logical_not(inside))
        def _():
            for halo in halos:
                halo[...] = jnp.zeros(halo.shape, jnp.float32)

    row = lax.broadcasted_iota(jnp.int32, (ny, nz), 0)
    lane = lax.broadcasted_iota(jnp.int32, (ny, nz), 1)
    first_row, last_row = row == 0, row == ny - 1
    last_lane = lane == nz - 1
    edge_lane = (lane == 0) | last_lane

    def remote(src, dst, send, recv, partner):
        return pltpu.make_async_remote_copy(
            src_ref=src, dst_ref=dst, send_sem=send, recv_sem=recv,
            device_id=partner, device_id_type=MESH,
        )

    def start_faces(up, down, has_lo, has_hi):
        @pl.when(has_hi)
        def _():
            for copy in up:
                copy.start()

        @pl.when(has_lo)
        def _():
            for copy in down:
                copy.start()

    def finish_faces(up, down, has_lo, has_hi):
        @pl.when(has_hi)
        def _():
            for copy in up:
                copy.wait_send()
            for copy in down:
                copy.wait_recv()

        @pl.when(has_lo)
        def _():
            for copy in down:
                copy.wait_send()
            for copy in up:
                copy.wait_recv()

    def faces_y(ylo, yhi, rlo, rhi, send, recv):
        return (
            [remote(yhi, rlo, send.at[0], recv.at[0], (gx, up_y))],
            [remote(ylo, rhi, send.at[1], recv.at[1], (gx, down_y))],
            has_lo_y, has_hi_y,
        )

    def faces_x(field, rlo, rhi, send, recv):
        return (
            [remote(field.at[:, nx - 1], rlo, send.at[2], recv.at[2], (up_x, gy))],
            [remote(field.at[:, 0], rhi, send.at[3], recv.at[3], (down_x, gy))],
            has_lo_x, has_hi_x,
        )

    for load in loads:
        load.wait()

    def properties(x, carry):
        label = LABEL[x]
        stiffness = (
            pick(rigidity, label)
            * (1.0 - 0.7 * YIELD[x].astype(jnp.float32))
            * (0.05 + 0.95 * PRINT[x].astype(jnp.float32))
        )
        half = 0.5 * stiffness
        H[x] = half
        TS[x] = pick(dilatation, label) * (0.5 + WARM[x]) * half
        half_c = 0.5 * pick(diffusivity, label)
        S3[2, x] = half_c
        at = pl.ds(x, 1)
        for c in range(3):
            y1_lo[c, at, :] = B[c, x, 0:1, :]
            y1_hi[c, at, :] = B[c, x, ny - 1 : ny, :]
        y1_lo[3, at, :] = half[0:1, :]
        y1_hi[3, at, :] = half[ny - 1 : ny, :]
        y3_lo[2, at, :] = half_c[0:1, :]
        y3_hi[2, at, :] = half_c[ny - 1 : ny, :]
        return carry

    lax.fori_loop(0, nx, properties, 0)

    pl.semaphore_wait(barrier, len(greeted))

    copies1y = faces_y(y1_lo, y1_hi, ry1_lo, ry1_hi, send1, recv1)
    fields = pl.ds(0, 3)
    copies1x = (
        [
            remote(B.at[:, nx - 1], rx1_lo.at[fields], send1.at[2], recv1.at[2], (up_x, gy)),
            remote(H.at[nx - 1], rx1_lo.at[3], send1.at[4], recv1.at[4], (up_x, gy)),
        ],
        [
            remote(B.at[:, 0], rx1_hi.at[fields], send1.at[3], recv1.at[3], (down_x, gy)),
            remote(H.at[0], rx1_hi.at[3], send1.at[5], recv1.at[5], (down_x, gy)),
        ],
        has_lo_x, has_hi_x,
    )
    start_faces(*copies1y)
    start_faces(*copies1x)

    def next_y(plane):
        return pltpu.roll(plane, ny - 1, 0)

    def prev_y(plane):
        return pltpu.roll(plane, 1, 0)

    def next_z(plane):
        return pltpu.roll(plane, nz - 1, 1)

    def prev_z(plane):
        return pltpu.roll(plane, 1, 1)

    def inflow(field, c, x, here, wxm, wxp, wy, wz):
        total = wxp * (field[c, jnp.minimum(x + 1, nx - 1)] - here)
        total += wxm * (field[c, jnp.maximum(x - 1, 0)] - here)
        flux = wy * (next_y(here) - here)
        total += flux - prev_y(flux)
        flux = wz * (next_z(here) - here)
        return total + (flux - prev_z(flux))

    def weights_yz(half):
        wy = jnp.where(last_row, 0.0, half + next_y(half))
        wz = jnp.where(last_lane, 0.0, half + next_z(half))
        return wy, wz

    def weights_x(x, half):
        return half + H[jnp.maximum(x - 1, 0)], half + H[jnp.minimum(x + 1, nx - 1)]

    zero = jnp.zeros((8, 128), jnp.float32)

    def first_image(x, carry):
        bu, uu = carry
        at = pl.ds(x, 1)
        half = H[x]
        wxm, wxp = weights_x(x, half)
        wy, wz = weights_yz(half)
        diag = 0.5 + jnp.where(edge_lane, half, 0.0)
        WY[x], WZ[x], D[x] = wy, wz, diag
        for c in range(3):
            here = B[c, x]
            image = diag * here - inflow(B, c, x, here, wxm, wxp, wy, wz)
            U[c, x] = image
            y2_lo[c, at, :] = image[0:1, :]
            y2_hi[c, at, :] = image[ny - 1 : ny, :]
            bu += fold(here * image)
            uu += fold(image * image)
        return bu, uu

    bu, uu = lax.fori_loop(0, nx, first_image, (zero, zero))

    finish_faces(*copies1x)
    for x, halo in ((0, rx1_lo), (nx - 1, rx1_hi)):
        weight = H[x] + halo[3]
        for c in range(3):
            here, image = B[c, x], U[c, x]
            more = weight * (here - halo[c])
            bu += fold(here * more)
            uu += fold(more * (2.0 * image + more))
            image += more
            U[c, x] = image
            y2_lo[c, x : x + 1, :] = image[0:1, :]
            y2_hi[c, x : x + 1, :] = image[ny - 1 : ny, :]
    finish_faces(*copies1y)
    for face, image, halo in ((y1_lo, y2_lo, ry1_lo), (y1_hi, y2_hi, ry1_hi)):
        weight = face[3] + halo[3]
        for c in range(3):
            more = weight * (face[c] - halo[c])
            bu += fold(face[c] * more)
            uu += fold(more * (2.0 * image[c] + more))
            image[c] = image[c] + more

    copies2y = faces_y(y2_lo, y2_hi, ry2_lo, ry2_hi, send2, recv2)
    start_faces(*copies2y)

    def set_rows(x, carry):
        at = pl.ds(x, 1)
        for c in range(3):
            U[c, x, 0:1, :] = y2_lo[c, at, :]
            U[c, x, ny - 1 : ny, :] = y2_hi[c, at, :]
        return carry

    lax.fori_loop(0, nx, set_rows, 0)
    copies2x = faces_x(U, rx2_lo, rx2_hi, send2, recv2)
    start_faces(*copies2x)

    def everywhere(tile):
        total = jnp.sum(jnp.sum(tile, axis=0, keepdims=True), axis=1, keepdims=True)
        return jnp.broadcast_to(total, (1, 128))

    weight = everywhere(uu)
    sigma = everywhere(bu) / jnp.where(weight > 0.0, weight, 1.0)
    sigma_all = jnp.broadcast_to(sigma[:, 0:1], (ny, nz))

    def second_image(x, carry):
        uu, rr, ru, rv, uv = carry
        half = H[x]
        wxm, wxp = weights_x(x, half)
        wy, wz, diag = WY[x], WZ[x], D[x]
        for c in range(3):
            here = U[c, x]
            image = diag * here - inflow(U, c, x, here, wxm, wxp, wy, wz)
            rest = B[c, x] - sigma_all * here
            uu += fold(here * here)
            rr += fold(rest * rest)
            ru += fold(rest * here)
            rv += fold(rest * image)
            uv += fold(here * image)
        return uu, rr, ru, rv, uv

    uu, rr, ru, rv, uv = lax.fori_loop(0, nx, second_image, (zero,) * 5)

    def source_of(field, xlo, xhi, rlo, rhi, out, ylo, yhi):
        def body(x, below, above):
            at = pl.ds(x, 1)
            mid, last = field[1, x], field[2, x]
            div = above - below
            div += jnp.where(last_row, rhi[1, at, :], next_y(mid))
            div -= jnp.where(first_row, rlo[1, at, :], prev_y(mid))
            div += jnp.where(last_lane, 0.0, next_z(last)) - jnp.where(lane == 0, 0.0, prev_z(last))
            source = -TS[x] * div
            S3[out, x] = source
            ylo[out, at, :] = source[0:1, :]
            yhi[out, at, :] = source[ny - 1 : ny, :]

        def inner(x, carry):
            body(x, field[0, x - 1], field[0, x + 1])
            return carry

        body(0, xlo[0], field[0, 1])
        lax.fori_loop(1, nx - 1, inner, 0)
        body(nx - 1, field[0, nx - 2], xhi[0])

    source_of(B, rx1_lo, rx1_hi, ry1_lo, ry1_hi, 0, y3_lo, y3_hi)

    finish_faces(*copies2x)
    for x, halo, stiff in ((0, rx2_lo, rx1_lo), (nx - 1, rx2_hi, rx1_hi)):
        weight = H[x] + stiff[3]
        for c in range(3):
            here = U[c, x]
            more = weight * (here - halo[c])
            rv += fold((B[c, x] - sigma_all * here) * more)
            uv += fold(here * more)
    finish_faces(*copies2y)
    sigma_face = jnp.broadcast_to(sigma[:, 0:1], (nx, nz))
    for face, image, halo, stiff in ((y1_lo, y2_lo, ry2_lo, ry1_lo), (y1_hi, y2_hi, ry2_hi, ry1_hi)):
        weight = face[3] + stiff[3]
        for c in range(3):
            here = image[c]
            more = weight * (here - halo[c])
            rv += fold((face[c] - sigma_face * here) * more)
            uv += fold(here * more)

    def lanes(tile):
        return jnp.sum(tile, axis=0, keepdims=True)

    def pack(parts):
        index = lax.broadcasted_iota(jnp.int32, (8, 128), 0)
        tile = jnp.zeros((8, 128), jnp.float32)
        for i, part in enumerate(parts):
            tile = jnp.where(index == i, jnp.broadcast_to(part, (8, 128)), tile)
        return tile

    def merge(tiles):
        rows = [[tile[i : i + 1, :] for i in range(7)] for tile in tiles]
        weight = sum(r[6] for r in rows)
        sigma = sum(r[6] * r[5] for r in rows) / jnp.where(weight > 0.0, weight, 1.0)
        out = [0.0] * 5
        for uu, rr, ru, rv, uv, own, _ in rows:
            tau = own - sigma
            shifted = (
                uu, rr + tau * (2.0 * ru + tau * uu), ru + tau * uu, rv + tau * uv, uv,
            )
            out = [a + b for a, b in zip(out, shifted)]
        return out + [sigma, weight]

    weight = everywhere(uu)
    state = [lanes(m) for m in (uu, rr, ru, rv, uv)] + [sigma, weight]

    def reduce_start(stage, state):
        base = sum(len(s) for s in stages[:stage])
        own = sums.at[base + stage]
        sums[base + stage] = pack(state)
        copies = []
        for k, partner in enumerate(stages[stage]):
            copies.append(
                remote(own, sums.at[base + stage + 1 + k], send_r.at[base + k], recv_r.at[base + k], partner)
            )
        for copy in copies:
            copy.start()
        return copies

    def reduce_finish(stage, copies):
        base = sum(len(s) for s in stages[:stage]) + stage
        for copy in copies:
            copy.wait()
        return merge([sums[base + k] for k in range(len(copies) + 1)])

    pending = reduce_start(0, state)
    source_of(U, rx2_lo, rx2_hi, ry2_lo, ry2_hi, 1, y3_lo, y3_hi)
    copies3y = faces_y(y3_lo, y3_hi, ry3_lo, ry3_hi, send3, recv3)
    copies3x = faces_x(S3, rx3_lo, rx3_hi, send3, recv3)
    start_faces(*copies3y)
    start_faces(*copies3x)
    state = reduce_finish(0, pending)
    pending = reduce_start(1, state)

    def conduct(x, carry):
        half = S3[2, x]
        wxm = half + S3[2, jnp.maximum(x - 1, 0)]
        wxp = half + S3[2, jnp.minimum(x + 1, nx - 1)]
        wy, wz = weights_yz(half)
        diag = 1.0 - 0.15 * jnp.where(edge_lane, half, 0.0)
        for c in range(2):
            here = S3[c, x]
            T[c, x] = diag * here + 0.15 * inflow(S3, c, x, here, wxm, wxp, wy, wz)
        return carry

    lax.fori_loop(0, nx, conduct, 0)
    state = reduce_finish(1, pending)
    pending = reduce_start(2, state)

    finish_faces(*copies3x)
    for x, halo in ((0, rx3_lo), (nx - 1, rx3_hi)):
        weight = 0.15 * (S3[2, x] + halo[2])
        for c in range(2):
            T[c, x] = T[c, x] + weight * (halo[c] - S3[c, x])
    finish_faces(*copies3y)
    for face, halo in ((y3_lo, ry3_lo), (y3_hi, ry3_hi)):
        weight = 0.15 * (face[2] + halo[2])
        for c in range(2):
            halo[c] = weight * (halo[c] - face[c])

    def add_rows(x, carry):
        at = pl.ds(x, 1)
        for c in range(2):
            T[c, x, 0:1, :] = T[c, x, 0:1, :] + ry3_lo[c, at, :]
            T[c, x, ny - 1 : ny, :] = T[c, x, ny - 1 : ny, :] + ry3_hi[c, at, :]
        return carry

    lax.fori_loop(0, nx, add_rows, 0)
    state = reduce_finish(2, pending)

    uu, rr, ru, rv, uv, sigma = [
        jnp.sum(part, axis=1, keepdims=True) for part in state[:5]
    ] + [state[5][:, 0:1]]
    energy = ru + sigma * uu
    norm = rr + sigma * (2.0 * ru + sigma * uu)
    step0 = norm / energy
    tau = sigma - step0
    norm1 = rr + tau * (2.0 * ru + tau * uu)
    ru, rv = ru + tau * uu, rv + tau * uv
    ratio = norm1 / norm
    curve = (ru - step0 * rv) + ratio * (2.0 * ru + ratio * energy)
    step1 = norm1 / curve
    coef_out[0:1, :] = jnp.broadcast_to(step0 + step1 * (1.0 + ratio), (1, 128))
    coef_out[1:2, :] = jnp.broadcast_to(-step1 * step0, (1, 128))


def combine(coef, b, u, t, x_out, th_out):
    coef_b = jnp.broadcast_to(coef[0:1, 0:1], x_out.shape[2:])
    coef_u = jnp.broadcast_to(coef[1:2, 0:1], x_out.shape[2:])
    for x in range(th_out.shape[0]):
        for c in range(3):
            x_out[c, x] = coef_b * b[c, x] + coef_u * u[c, x]
        th_out[x] = coef_b * t[0, x] + coef_u * t[1, x]


def per_device(*args):
    b = args[0]
    _, nx, ny, nz = b.shape
    gx_size, gy_size = lax.axis_size("gx"), lax.axis_size("gy")
    partners = gx_size - 1 + gy_size // RING_X - 1 + RING_X - 1
    f32 = jnp.float32
    block = (nx, ny, nz)
    hbm, vmem = (pl.BlockSpec(memory_space=m) for m in (pltpu.HBM, pltpu.VMEM))
    dma = pltpu.SemaphoreType.DMA
    scratch = [pltpu.VMEM((3,) + block, f32)]
    scratch += [pltpu.VMEM(block, t) for t in [f32] * 2 + [jnp.int32] * 3 + [f32] * 4]
    scratch += [pltpu.VMEM((3,) + block, f32)]
    for fields in (4, 3, 3):
        scratch += [pltpu.VMEM((fields, nx, nz), f32)] * 4
        scratch += [pltpu.VMEM((fields, ny, nz), f32)] * 2
    scratch += [pltpu.VMEM((partners + 3, 8, 128), f32)]
    scratch += [pltpu.SMEM((4,), f32)] * 3
    scratch += [dma((8,))] + [dma((6,))] * 2 + [dma((4,))] * 4 + [dma((partners,))] * 2
    u, t, coef = pl.pallas_call(
        functools.partial(kernel, gx_size, gy_size),
        out_shape=(
            jax.ShapeDtypeStruct((3,) + block, f32),
            jax.ShapeDtypeStruct((2,) + block, f32),
            jax.ShapeDtypeStruct((8, 128), f32),
        ),
        in_specs=[hbm] * 8,
        out_specs=(vmem, vmem, vmem),
        scratch_shapes=scratch,
        compiler_params=pltpu.CompilerParams(
            collective_id=0, has_side_effects=True, vmem_limit_bytes=40 * 1024 * 1024
        ),
        name="adjoint",
    )(*[pltpu.with_memory_space_constraint(arg, pltpu.HBM) for arg in args])
    return pl.pallas_call(
        combine,
        grid=(4,),
        out_shape=(
            jax.ShapeDtypeStruct((3,) + block, f32), jax.ShapeDtypeStruct(block, f32),
        ),
        in_specs=[
            pl.BlockSpec((8, 128), lambda i: (0, 0)),
            pl.BlockSpec((3, nx // 4, ny, nz), lambda i: (0, i, 0, 0)),
            pl.BlockSpec((3, nx // 4, ny, nz), lambda i: (0, i, 0, 0)),
            pl.BlockSpec((2, nx // 4, ny, nz), lambda i: (0, i, 0, 0)),
        ],
        out_specs=(
            pl.BlockSpec((3, nx // 4, ny, nz), lambda i: (0, i, 0, 0)),
            pl.BlockSpec((nx // 4, ny, nz), lambda i: (i, 0, 0)),
        ),
        compiler_params=pltpu.CompilerParams(vmem_limit_bytes=24 * 1024 * 1024),
        name="combine",
    )(coef, b, u, t)


def solution(mesh):
    in_specs = (
        P(None, "gx", "gy", None),
        P("gx", "gy", None),
        P("gx", "gy", None),
        P("gx", "gy", None),
        P("gx", "gy", None),
        P(),
        P(),
        P(),
    )
    out_specs = (P(None, "gx", "gy", None), P("gx", "gy", None))
    return jax.shard_map(
        per_device, mesh=mesh, in_specs=in_specs, out_specs=out_specs, check_vma=False
    )
```

time: 50 us -> 35.5 us (0.71)
  local copies, waits for them, and re-layouts: 9.47 us -> 0.01 us
  Pallas kernels: 39.6 us -> 34.8 us
    unnamed x18 -> x2, local copies, waits for them, and re-layouts: 9.47 us -> 0.01 us
    pallas_call x1, Pallas kernels: 39.6 us -> 32.6 us  [per_device(): pl.pallas_call(functools.partial(kernel, gx_size, gy_size), out_shape=(ja...]
    pallas_call x0 -> x1, Pallas kernels: none -> 2.19 us  [per_device(): pl.pallas_call(combine, grid=(4,), out_shape=(jax.ShapeDtypeStruct((3,) +...]
where the time goes in v2:
time: 35.5 us; the launch traced here: 35.4 us
  Pallas kernels  34.8 us (98%)
  between operations  0.66 us (2%)
    pallas_call x1, Pallas kernels, per_device(): pl.pallas_call(functools.partial(kernel, gx_size, gy_size), out_shape=(ja...  32.6 us
    pallas_call x1, Pallas kernels, per_device(): pl.pallas_call(combine, grid=(4,), out_shape=(jax.ShapeDtypeStruct((3,) +...  2.19 us

profile of v2, /device:TPU:1, one launch (start us, length us, event | category | flops | bytes accessed | tf_op | source)
XLA Modules:
  0.0 35.4 jit_solution(6755120973366962876)
XLA Ops:
  0.6 0.0 copy-start
  0.6 32.6 %adjoint.1 = (f32[3,16,16,512]{3,2,1,0:T(8,128)S(1)}, f32[2,16,16,512]{3,2,1,0:T(8,128)S(1)}, f32[8,128]{1,0:T(8,128)S(1)}) custom-call(f32[3,16,16,512]{3,2,1,0:T(8,128)} %b.1, f32[16,16,512]{2,1,0:T(8,128)} %warm_hbm.1, s32[16,16,512]{2,1,0:T(8,128)} %yield_hbm.1, s32[16,16,512]{2,1,0:T(8,128)} %print_hbm.1, s32[16,16,512]{2,1,0:T(8,128)} %label_hbm.1, ...), custom_call_target="tpu_custom_call" | custom-call | tf_op jit(solution)/shard_map/adjoint/pallas_call | solution.py:475
  33.2 0.0 copy-done
  33.2 2.2 %combine.1 = (f32[3,16,16,512]{3,2,1,0:T(8,128)}, f32[16,16,512]{2,1,0:T(8,128)}) custom-call(f32[8,128]{1,0:T(8,128)S(1)} %get-tuple-element.5.coef, f32[3,16,16,512]{3,2,1,0:T(8,128)S(1)} %copy-done, f32[3,16,16,512]{3,2,1,0:T(8,128)S(1)} %get-tuple-element.6.u, f32[2,16,16,512]{3,2,1,0:T(8,128)S(1)} %get-tuple-element.7.t), custom_call_target="tpu_custom_call" | custom-call | tf_op jit(solution)/shard_map/combine/pallas_call | solution.py:490
Async XLA Ops:
  0.6 32.6 %copy-start = (f32[3,16,16,512]{3,2,1,0:T(8,128)S(1)}, f32[3,16,16,512]{3,2,1,0:T(8,128)}, u32[]{:S(2)}) copy-start(f32[3,16,16,512]{3,2,1,0:T(8,128)} %b.1) | copy-start | bytes 4718596

commit v3 on v2

--- a/solution.py
+++ b/solution.py
@@ -1,4 +1,5 @@
 import functools
+import itertools
 
 import jax
 import jax.numpy as jnp
@@ -25,6 +26,28 @@
             part = plane[i : i + 8, j : j + 128]
             total = part if total is None else total + part
     return total
+
+
+GROUPS = ("cz", "xy")
+PIECES = 2
+
+
+def offset_partners(group, gx, gy, gx_size, gy_size):
+    sizes = {"c": 2, "y": gx_size // 2, "z": gy_size // RING_X, "x": RING_X}
+    place = {"c": gx % 2, "y": gx // 2, "z": gy // RING_X, "x": gy % RING_X}
+    partners = []
+
+    def hops(offsets):
+        return sum(min(o, sizes[axis] - o) for axis, o in zip(group, offsets))
+
+    every = itertools.product(*[range(sizes[axis]) for axis in group])
+    for offsets in sorted(every, key=hops, reverse=True):
+        if any(offsets):
+            to = dict(place)
+            for axis, offset in zip(group, offsets):
+                to[axis] = (place[axis] + offset) % sizes[axis]
+            partners.append((to["y"] * 2 + to["c"], to["z"] * RING_X + to["x"]))
+    return partners
 
 
 def kernel(
@@ -47,17 +70,7 @@
     up_y, down_y = (gy + 1) % gy_size, (gy + gy_size - 1) % gy_size
     has_lo_x, has_hi_x = gx > 0, gx < gx_size - 1
     has_lo_y, has_hi_y = gy > 0, gy < gy_size - 1
-    stages = []
-    for stage, count in enumerate((gx_size, ring_z, RING_X)):
-        partners = []
-        for k in range(1, count):
-            if stage == 0:
-                partners.append(((gx + k) % gx_size, gy))
-            elif stage == 1:
-                partners.append((gx, ((gz + k) % ring_z) * RING_X + gq))
-            else:
-                partners.append((gx, gz * RING_X + (gq + k) % RING_X))
-        stages.append(partners)
+    stages = [offset_partners(group, gx, gy, gx_size, gy_size) for group in GROUPS]
 
     loads = [
         pltpu.make_async_copy(rigidity_hbm, rigidity, load_sem.at[5]),
@@ -381,17 +394,15 @@
     def reduce_finish(stage, copies):
         base = sum(len(s) for s in stages[:stage]) + stage
         for copy in copies:
-            copy.wait()
+            copy.wait_recv()
         return merge([sums[base + k] for k in range(len(copies) + 1)])
 
-    pending = reduce_start(0, state)
+    pending0 = reduce_start(0, state)
     source_of(U, rx2_lo, rx2_hi, ry2_lo, ry2_hi, 1, y3_lo, y3_hi)
     copies3y = faces_y(y3_lo, y3_hi, ry3_lo, ry3_hi, send3, recv3)
     copies3x = faces_x(S3, rx3_lo, rx3_hi, send3, recv3)
     start_faces(*copies3y)
     start_faces(*copies3x)
-    state = reduce_finish(0, pending)
-    pending = reduce_start(1, state)
 
     def conduct(x, carry):
         half = S3[2, x]
@@ -405,8 +416,8 @@
         return carry
 
     lax.fori_loop(0, nx, conduct, 0)
-    state = reduce_finish(1, pending)
-    pending = reduce_start(2, state)
+    state = reduce_finish(0, pending0)
+    pending1 = reduce_start(1, state)
 
     finish_faces(*copies3x)
     for x, halo in ((0, rx3_lo), (nx - 1, rx3_hi)):
@@ -427,7 +438,11 @@
         return carry
 
     lax.fori_loop(0, nx, add_rows, 0)
-    state = reduce_finish(2, pending)
+    for copy in pending0:
+        copy.wait_send()
+    state = reduce_finish(1, pending1)
+    for copy in pending1:
+        copy.wait_send()
 
     uu, rr, ru, rv, uv, sigma = [
         jnp.sum(part, axis=1, keepdims=True) for part in state[:5]
@@ -445,20 +460,40 @@
     coef_out[1:2, :] = jnp.broadcast_to(-step1 * step0, (1, 128))
 
 
-def combine(coef, b, u, t, x_out, th_out):
-    coef_b = jnp.broadcast_to(coef[0:1, 0:1], x_out.shape[2:])
-    coef_u = jnp.broadcast_to(coef[1:2, 0:1], x_out.shape[2:])
-    for x in range(th_out.shape[0]):
-        for c in range(3):
-            x_out[c, x] = coef_b * b[c, x] + coef_u * u[c, x]
-        th_out[x] = coef_b * t[0, x] + coef_u * t[1, x]
+def combine(coef, b, u, t, x_hbm, th_hbm, x_out, th_out, sem):
+    _, nx, ny, nz = b.shape
+    coef_b = jnp.broadcast_to(coef[0:1, 0:1], (ny, nz))
+    coef_u = jnp.broadcast_to(coef[1:2, 0:1], (ny, nz))
+    copies = []
+    chunk = nx // PIECES
+    for piece in range(PIECES):
+        for c in range(4):
+            here = piece * chunk
+
+            def one(x, carry):
+                if c < 3:
+                    x_out[c, x] = coef_b * b[c, x] + coef_u * u[c, x]
+                else:
+                    th_out[x] = coef_b * t[0, x] + coef_u * t[1, x]
+                return carry
+
+            lax.fori_loop(here, here + chunk, one, 0, unroll=True)
+            planes = pl.ds(here, chunk)
+            if c < 3:
+                src, dst = x_out.at[c, planes], x_hbm.at[c, planes]
+            else:
+                src, dst = th_out.at[planes], th_hbm.at[planes]
+            copies.append(pltpu.make_async_copy(src, dst, sem.at[len(copies)]))
+            copies[-1].start()
+    for copy in copies:
+        copy.wait()
 
 
 def per_device(*args):
     b = args[0]
     _, nx, ny, nz = b.shape
     gx_size, gy_size = lax.axis_size("gx"), lax.axis_size("gy")
-    partners = gx_size - 1 + gy_size // RING_X - 1 + RING_X - 1
+    partners = sum(len(offset_partners(group, 0, 0, gx_size, gy_size)) for group in GROUPS)
     f32 = jnp.float32
     block = (nx, ny, nz)
     hbm, vmem = (pl.BlockSpec(memory_space=m) for m in (pltpu.HBM, pltpu.VMEM))
@@ -469,7 +504,7 @@
     for fields in (4, 3, 3):
         scratch += [pltpu.VMEM((fields, nx, nz), f32)] * 4
         scratch += [pltpu.VMEM((fields, ny, nz), f32)] * 2
-    scratch += [pltpu.VMEM((partners + 3, 8, 128), f32)]
+    scratch += [pltpu.VMEM((partners + len(GROUPS), 8, 128), f32)]
     scratch += [pltpu.SMEM((4,), f32)] * 3
     scratch += [dma((8,))] + [dma((6,))] * 2 + [dma((4,))] * 4 + [dma((partners,))] * 2
     u, t, coef = pl.pallas_call(
@@ -489,21 +524,15 @@
     )(*[pltpu.with_memory_space_constraint(arg, pltpu.HBM) for arg in args])
     return pl.pallas_call(
         combine,
-        grid=(4,),
         out_shape=(
             jax.ShapeDtypeStruct((3,) + block, f32), jax.ShapeDtypeStruct(block, f32),
         ),
-        in_specs=[
-            pl.BlockSpec((8, 128), lambda i: (0, 0)),
-            pl.BlockSpec((3, nx // 4, ny, nz), lambda i: (0, i, 0, 0)),
-            pl.BlockSpec((3, nx // 4, ny, nz), lambda i: (0, i, 0, 0)),
-            pl.BlockSpec((2, nx // 4, ny, nz), lambda i: (0, i, 0, 0)),
+        in_specs=[vmem] * 4,
+        out_specs=(hbm, hbm),
+        scratch_shapes=[
+            pltpu.VMEM((3,) + block, f32), pltpu.VMEM(block, f32), dma((4 * PIECES,)),
         ],
-        out_specs=(
-            pl.BlockSpec((3, nx // 4, ny, nz), lambda i: (0, i, 0, 0)),
-            pl.BlockSpec((nx // 4, ny, nz), lambda i: (i, 0, 0)),
-        ),
-        compiler_params=pltpu.CompilerParams(vmem_limit_bytes=24 * 1024 * 1024),
+        compiler_params=pltpu.CompilerParams(vmem_limit_bytes=16 * 1024 * 1024),
         name="combine",
     )(coef, b, u, t)
 

time: 35.5 us -> 33.4 us (0.941)
  Pallas kernels: 34.8 us -> 32.6 us
    pallas_call x1, Pallas kernels: 32.6 us -> 31.2 us  [per_device(): pl.pallas_call(functools.partial(kernel, gx_size, gy_size), out_shape=(ja...]
    pallas_call x1, Pallas kernels: 2.19 us -> 1.45 us  [per_device(): pl.pallas_call(combine, out_shape=(jax.ShapeDtypeStruct((3,) + block, f32...]
where the time goes in v3:
time: 33.4 us; the launch traced here: 33.3 us
  Pallas kernels  32.6 us (98%)
  between operations  0.66 us (2%)
    pallas_call x1, Pallas kernels, per_device(): pl.pallas_call(functools.partial(kernel, gx_size, gy_size), out_shape=(ja...  31.2 us
    pallas_call x1, Pallas kernels, per_device(): pl.pallas_call(combine, out_shape=(jax.ShapeDtypeStruct((3,) + block, f32...  1.45 us

profile of v3, /device:TPU:1, one launch (start us, length us, event | category | flops | bytes accessed | tf_op | source)
XLA Modules:
  0.0 33.3 jit_solution(11780638685435795232)
XLA Ops:
  0.6 0.0 copy-start
  0.6 31.2 %adjoint.1 = (f32[3,16,16,512]{3,2,1,0:T(8,128)S(1)}, f32[2,16,16,512]{3,2,1,0:T(8,128)S(1)}, f32[8,128]{1,0:T(8,128)S(1)}) custom-call(f32[3,16,16,512]{3,2,1,0:T(8,128)} %b.1, f32[16,16,512]{2,1,0:T(8,128)} %warm_hbm.1, s32[16,16,512]{2,1,0:T(8,128)} %yield_hbm.1, s32[16,16,512]{2,1,0:T(8,128)} %print_hbm.1, s32[16,16,512]{2,1,0:T(8,128)} %label_hbm.1, ...), custom_call_target="tpu_custom_call" | custom-call | tf_op jit(solution)/shard_map/adjoint/pallas_call | solution.py:510
  31.8 0.0 copy-done
  31.8 1.4 %combine.1 = (f32[3,16,16,512]{3,2,1,0:T(8,128)}, f32[16,16,512]{2,1,0:T(8,128)}) custom-call(f32[8,128]{1,0:T(8,128)S(1)} %get-tuple-element.5.coef, f32[3,16,16,512]{3,2,1,0:T(8,128)S(1)} %copy-done, f32[3,16,16,512]{3,2,1,0:T(8,128)S(1)} %get-tuple-element.6.u, f32[2,16,16,512]{3,2,1,0:T(8,128)S(1)} %get-tuple-element.7.t), custom_call_target="tpu_custom_call" | custom-call | tf_op jit(solution)/shard_map/combine/pallas_call | solution.py:525
Async XLA Ops:
  0.6 31.2 %copy-start = (f32[3,16,16,512]{3,2,1,0:T(8,128)S(1)}, f32[3,16,16,512]{3,2,1,0:T(8,128)}, u32[]{:S(2)}) copy-start(f32[3,16,16,512]{3,2,1,0:T(8,128)} %b.1) | copy-start | bytes 4718596

commit v4 on v3

--- a/solution.py
+++ b/solution.py
@@ -56,11 +56,11 @@
     U, T, coef_out,
     B, H, WARM, YIELD, PRINT, LABEL, TS, WY, WZ, D, S3,
     y1_lo, y1_hi, ry1_lo, ry1_hi, rx1_lo, rx1_hi,
-    y2_lo, y2_hi, ry2_lo, ry2_hi, rx2_lo, rx2_hi,
+    y2_lo, y2_hi, ry2_lo, ry2_hi, rx2_lo, rx2_hi, x2_lo, x2_hi, yu_lo, yu_hi,
     y3_lo, y3_hi, ry3_lo, ry3_hi, rx3_lo, rx3_hi,
-    sums,
+    corner, rcorner, sums,
     rigidity, dilatation, diffusivity,
-    load_sem, send1, recv1, send2, recv2, send3, recv3, send_r, recv_r,
+    load_sem, send_c, recv_c, send1, recv1, send2, recv2, send3, recv3, send_r, recv_r,
 ):
     _, nx, ny, nz = b_hbm.shape
     gx, gy = lax.axis_index("gx"), lax.axis_index("gy")
@@ -79,18 +79,29 @@
         pltpu.make_async_copy(label_hbm, LABEL, load_sem.at[0]),
         pltpu.make_async_copy(yield_hbm, YIELD, load_sem.at[1]),
         pltpu.make_async_copy(print_hbm, PRINT, load_sem.at[2]),
+        pltpu.make_async_copy(b_hbm, B, load_sem.at[4]),
         pltpu.make_async_copy(warm_hbm, WARM, load_sem.at[3]),
-        pltpu.make_async_copy(b_hbm, B, load_sem.at[4]),
     ]
     for load in loads:
         load.start()
 
     barrier = pltpu.get_barrier_semaphore()
-    greeted = [(up_x, gy), (down_x, gy), (gx, up_y), (gx, down_y)]
-    for partners in stages:
-        greeted += partners
-    for partner in greeted:
+    diagonal = [(x, y) for x in (down_x, up_x) for y in (down_y, up_y)]
+    inside_c = [x & y for x in (has_lo_x, has_hi_x) for y in (has_lo_y, has_hi_y)]
+    always = stages[0] + stages[1]
+    greeted = list(zip(
+        [(up_x, gy), (down_x, gy), (gx, up_y), (gx, down_y)] + diagonal,
+        [has_hi_x, has_lo_x, has_hi_y, has_lo_y] + inside_c,
+    ))
+
+    def greet(partner):
         pl.semaphore_signal(barrier, inc=1, device_id=partner, device_id_type=MESH)
+
+    for partner in always:
+        greet(partner)
+    for partner, inside in greeted:
+        pl.when(inside)(functools.partial(greet, partner))
+    answers = len(always) + sum(inside.astype(jnp.int32) for _, inside in greeted)
 
     for inside, halos in (
         (has_lo_x, (rx1_lo, rx2_lo, rx3_lo)),
@@ -103,6 +114,11 @@
             for halo in halos:
                 halo[...] = jnp.zeros(halo.shape, jnp.float32)
 
+    for k, inside in enumerate(inside_c):
+        @pl.when(jnp.logical_not(inside))
+        def _():
+            rcorner[k] = jnp.zeros(rcorner.shape[1:], jnp.float32)
+
     row = lax.broadcasted_iota(jnp.int32, (ny, nz), 0)
     lane = lax.broadcasted_iota(jnp.int32, (ny, nz), 1)
     first_row, last_row = row == 0, row == ny - 1
@@ -155,7 +171,7 @@
             has_lo_x, has_hi_x,
         )
 
-    for load in loads:
+    for load in loads[:-1]:
         load.wait()
 
     def properties(x, carry):
@@ -167,22 +183,32 @@
         )
         half = 0.5 * stiffness
         H[x] = half
-        TS[x] = pick(dilatation, label) * (0.5 + WARM[x]) * half
-        half_c = 0.5 * pick(diffusivity, label)
-        S3[2, x] = half_c
         at = pl.ds(x, 1)
         for c in range(3):
             y1_lo[c, at, :] = B[c, x, 0:1, :]
             y1_hi[c, at, :] = B[c, x, ny - 1 : ny, :]
         y1_lo[3, at, :] = half[0:1, :]
         y1_hi[3, at, :] = half[ny - 1 : ny, :]
-        y3_lo[2, at, :] = half_c[0:1, :]
-        y3_hi[2, at, :] = half_c[ny - 1 : ny, :]
         return carry
 
     lax.fori_loop(0, nx, properties, 0)
 
-    pl.semaphore_wait(barrier, len(greeted))
+    corners = [(x, y) for x in (0, nx - 1) for y in (0, ny - 1)]
+    for k, (x, y) in enumerate(corners):
+        for c in range(3):
+            corner[k, c : c + 1, :] = B[c, x, y : y + 1, :]
+        corner[k, 3:4, :] = H[x, y : y + 1, :]
+
+    pl.semaphore_wait(barrier, answers)
+
+    copies_c = [
+        remote(corner.at[k], rcorner.at[3 - k], send_c.at[k], recv_c.at[3 - k], partner)
+        for k, partner in enumerate(diagonal)
+    ]
+    for copy, inside in zip(copies_c, inside_c):
+        @pl.when(inside)
+        def _():
+            copy.start()
 
     copies1y = faces_y(y1_lo, y1_hi, ry1_lo, ry1_hi, send1, recv1)
     fields = pl.ds(0, 3)
@@ -250,6 +276,33 @@
 
     bu, uu = lax.fori_loop(0, nx, first_image, (zero, zero))
 
+    for c in range(3):
+        x2_lo[c], x2_hi[c] = U[c, 0], U[c, nx - 1]
+    copies2y = faces_y(y2_lo, y2_hi, ry2_lo, ry2_hi, send2, recv2)
+    copies2x = (
+        [remote(x2_hi, rx2_lo, send2.at[2], recv2.at[2], (up_x, gy))],
+        [remote(x2_lo, rx2_hi, send2.at[3], recv2.at[3], (down_x, gy))],
+        has_lo_x, has_hi_x,
+    )
+    start_faces(*copies2y)
+    start_faces(*copies2x)
+    for c in range(3):
+        yu_lo[c], yu_hi[c] = y2_lo[c], y2_hi[c]
+
+    loads[-1].wait()
+
+    def thermal_properties(x, carry):
+        label = LABEL[x]
+        TS[x] = pick(dilatation, label) * (0.5 + WARM[x]) * H[x]
+        half_c = 0.5 * pick(diffusivity, label)
+        S3[2, x] = half_c
+        at = pl.ds(x, 1)
+        y3_lo[2, at, :] = half_c[0:1, :]
+        y3_hi[2, at, :] = half_c[ny - 1 : ny, :]
+        return carry
+
+    lax.fori_loop(0, nx, thermal_properties, 0)
+
     finish_faces(*copies1x)
     for x, halo in ((0, rx1_lo), (nx - 1, rx1_hi)):
         weight = H[x] + halo[3]
@@ -260,10 +313,10 @@
             uu += fold(more * (2.0 * image + more))
             image += more
             U[c, x] = image
-            y2_lo[c, x : x + 1, :] = image[0:1, :]
-            y2_hi[c, x : x + 1, :] = image[ny - 1 : ny, :]
+            yu_lo[c, x : x + 1, :] = image[0:1, :]
+            yu_hi[c, x : x + 1, :] = image[ny - 1 : ny, :]
     finish_faces(*copies1y)
-    for face, image, halo in ((y1_lo, y2_lo, ry1_lo), (y1_hi, y2_hi, ry1_hi)):
+    for face, image, halo in ((y1_lo, yu_lo, ry1_lo), (y1_hi, yu_hi, ry1_hi)):
         weight = face[3] + halo[3]
         for c in range(3):
             more = weight * (face[c] - halo[c])
@@ -271,19 +324,14 @@
             uu += fold(more * (2.0 * image[c] + more))
             image[c] = image[c] + more
 
-    copies2y = faces_y(y2_lo, y2_hi, ry2_lo, ry2_hi, send2, recv2)
-    start_faces(*copies2y)
-
     def set_rows(x, carry):
         at = pl.ds(x, 1)
         for c in range(3):
-            U[c, x, 0:1, :] = y2_lo[c, at, :]
-            U[c, x, ny - 1 : ny, :] = y2_hi[c, at, :]
+            U[c, x, 0:1, :] = yu_lo[c, at, :]
+            U[c, x, ny - 1 : ny, :] = yu_hi[c, at, :]
         return carry
 
     lax.fori_loop(0, nx, set_rows, 0)
-    copies2x = faces_x(U, rx2_lo, rx2_hi, send2, recv2)
-    start_faces(*copies2x)
 
     def everywhere(tile):
         total = jnp.sum(jnp.sum(tile, axis=0, keepdims=True), axis=1, keepdims=True)
@@ -332,9 +380,30 @@
         lax.fori_loop(1, nx - 1, inner, 0)
         body(nx - 1, field[0, nx - 2], xhi[0])
 
-    source_of(B, rx1_lo, rx1_hi, ry1_lo, ry1_hi, 0, y3_lo, y3_hi)
+    for k, inside in enumerate(inside_c):
+        @pl.when(inside)
+        def _():
+            copies_c[k].wait_send()
+            copies_c[3 - k].wait_recv()
+
+    def complete(halo, field, own, low, high):
+        weight = own(3) + field[3]
+        for c in range(3):
+            halo[c] = halo[c] + weight * (field[c] - own(c))
+            for at, line in ((0, low), (field.shape[1] - 1, high)):
+                at = slice(at, at + 1)
+                edge = field[3, at, :] + rcorner[line, 3:4, :]
+                edge = edge * (field[c, at, :] - rcorner[line, c : c + 1, :])
+                halo[c, at, :] = halo[c, at, :] + edge
 
     finish_faces(*copies2x)
+    for x, inside, halo, field, low, high in (
+        (0, has_lo_x, rx2_lo, rx1_lo, 0, 1), (nx - 1, has_hi_x, rx2_hi, rx1_hi, 2, 3),
+    ):
+        @pl.when(inside)
+        def _():
+            complete(halo, field, lambda c: B[c, x] if c < 3 else H[x], low, high)
+
     for x, halo, stiff in ((0, rx2_lo, rx1_lo), (nx - 1, rx2_hi, rx1_hi)):
         weight = H[x] + stiff[3]
         for c in range(3):
@@ -343,8 +412,15 @@
             rv += fold((B[c, x] - sigma_all * here) * more)
             uv += fold(here * more)
     finish_faces(*copies2y)
+    for inside, halo, field, face, low, high in (
+        (has_lo_y, ry2_lo, ry1_lo, y1_lo, 0, 2), (has_hi_y, ry2_hi, ry1_hi, y1_hi, 1, 3),
+    ):
+        @pl.when(inside)
+        def _():
+            complete(halo, field, lambda c: face[c], low, high)
+
     sigma_face = jnp.broadcast_to(sigma[:, 0:1], (nx, nz))
-    for face, image, halo, stiff in ((y1_lo, y2_lo, ry2_lo, ry1_lo), (y1_hi, y2_hi, ry2_hi, ry1_hi)):
+    for face, image, halo, stiff in ((y1_lo, yu_lo, ry2_lo, ry1_lo), (y1_hi, yu_hi, ry2_hi, ry1_hi)):
         weight = face[3] + stiff[3]
         for c in range(3):
             here = image[c]
@@ -398,6 +474,7 @@
         return merge([sums[base + k] for k in range(len(copies) + 1)])
 
     pending0 = reduce_start(0, state)
+    source_of(B, rx1_lo, rx1_hi, ry1_lo, ry1_hi, 0, y3_lo, y3_hi)
     source_of(U, rx2_lo, rx2_hi, ry2_lo, ry2_hi, 1, y3_lo, y3_hi)
     copies3y = faces_y(y3_lo, y3_hi, ry3_lo, ry3_hi, send3, recv3)
     copies3x = faces_x(S3, rx3_lo, rx3_hi, send3, recv3)
@@ -504,9 +581,12 @@
     for fields in (4, 3, 3):
         scratch += [pltpu.VMEM((fields, nx, nz), f32)] * 4
         scratch += [pltpu.VMEM((fields, ny, nz), f32)] * 2
+        if len(scratch) == 11 + 12:
+            scratch += [pltpu.VMEM((3, ny, nz), f32)] * 2 + [pltpu.VMEM((3, nx, nz), f32)] * 2
+    scratch += [pltpu.VMEM((4, 8, nz), f32)] * 2
     scratch += [pltpu.VMEM((partners + len(GROUPS), 8, 128), f32)]
     scratch += [pltpu.SMEM((4,), f32)] * 3
-    scratch += [dma((8,))] + [dma((6,))] * 2 + [dma((4,))] * 4 + [dma((partners,))] * 2
+    scratch += [dma((8,))] + [dma((4,))] * 2 + [dma((6,))] * 2 + [dma((4,))] * 4 + [dma((partners,))] * 2
     u, t, coef = pl.pallas_call(
         functools.partial(kernel, gx_size, gy_size),
         out_shape=(

time: 33.4 us -> 32.9 us (0.985)
  Pallas kernels: 32.6 us -> 32.2 us
    pallas_call x1, Pallas kernels: 31.2 us -> 30.8 us  [per_device(): pl.pallas_call(functools.partial(kernel, gx_size, gy_size), out_shape=(ja...]
where the time goes in v4:
time: 32.9 us
  Pallas kernels  32.2 us (98%)
  between operations  0.66 us (2%)
    pallas_call x1, Pallas kernels, per_device(): pl.pallas_call(functools.partial(kernel, gx_size, gy_size), out_shape=(ja...  30.8 us
    pallas_call x1, Pallas kernels, per_device(): pl.pallas_call(combine, out_shape=(jax.ShapeDtypeStruct((3,) + block, f32...  1.45 us

profile of v4, /device:TPU:1, one launch (start us, length us, event | category | flops | bytes accessed | tf_op | source)
XLA Modules:
  0.0 32.9 jit_solution(11376284611746299894)
XLA Ops:
  0.6 0.0 copy-start
  0.6 30.8 %adjoint.1 = (f32[3,16,16,512]{3,2,1,0:T(8,128)S(1)}, f32[2,16,16,512]{3,2,1,0:T(8,128)S(1)}, f32[8,128]{1,0:T(8,128)S(1)}) custom-call(f32[3,16,16,512]{3,2,1,0:T(8,128)} %b.1, f32[16,16,512]{2,1,0:T(8,128)} %warm_hbm.1, s32[16,16,512]{2,1,0:T(8,128)} %yield_hbm.1, s32[16,16,512]{2,1,0:T(8,128)} %print_hbm.1, s32[16,16,512]{2,1,0:T(8,128)} %label_hbm.1, ...), custom_call_target="tpu_custom_call" | custom-call | tf_op jit(solution)/shard_map/adjoint/pallas_call | solution.py:590
  31.4 0.0 copy-done
  31.4 1.4 %combine.1 = (f32[3,16,16,512]{3,2,1,0:T(8,128)}, f32[16,16,512]{2,1,0:T(8,128)}) custom-call(f32[8,128]{1,0:T(8,128)S(1)} %get-tuple-element.5.coef, f32[3,16,16,512]{3,2,1,0:T(8,128)S(1)} %copy-done, f32[3,16,16,512]{3,2,1,0:T(8,128)S(1)} %get-tuple-element.6.u, f32[2,16,16,512]{3,2,1,0:T(8,128)S(1)} %get-tuple-element.7.t), custom_call_target="tpu_custom_call" | custom-call | tf_op jit(solution)/shard_map/combine/pallas_call | solution.py:605
Async XLA Ops:
  0.6 30.8 %copy-start = (f32[3,16,16,512]{3,2,1,0:T(8,128)S(1)}, f32[3,16,16,512]{3,2,1,0:T(8,128)}, u32[]{:S(2)}) copy-start(f32[3,16,16,512]{3,2,1,0:T(8,128)} %b.1) | copy-start | bytes 4718596

commit v5 on v4

--- a/solution.py
+++ b/solution.py
@@ -53,8 +53,8 @@
 def kernel(
     gx_size, gy_size,
     b_hbm, warm_hbm, yield_hbm, print_hbm, label_hbm, rigidity_hbm, dilatation_hbm, diffusivity_hbm,
-    U, T, coef_out,
-    B, H, WARM, YIELD, PRINT, LABEL, TS, WY, WZ, D, S3,
+    U, T, coef_out, B,
+    H, WARM, YIELD, PRINT, LABEL, TS, WY, WZ, D, S3,
     y1_lo, y1_hi, ry1_lo, ry1_hi, rx1_lo, rx1_hi,
     y2_lo, y2_hi, ry2_lo, ry2_hi, rx2_lo, rx2_hi, x2_lo, x2_hi, yu_lo, yu_hi,
     y3_lo, y3_hi, ry3_lo, ry3_hi, rx3_lo, rx3_hi,
@@ -331,18 +331,18 @@
             U[c, x, ny - 1 : ny, :] = yu_hi[c, at, :]
         return carry
 
-    lax.fori_loop(0, nx, set_rows, 0)
+    lax.fori_loop(0, nx, set_rows, 0, unroll=4)
 
     def everywhere(tile):
         total = jnp.sum(jnp.sum(tile, axis=0, keepdims=True), axis=1, keepdims=True)
         return jnp.broadcast_to(total, (1, 128))
 
-    weight = everywhere(uu)
-    sigma = everywhere(bu) / jnp.where(weight > 0.0, weight, 1.0)
+    total = everywhere(uu)
+    sigma = everywhere(bu) / jnp.where(total > 0.0, total, 1.0)
     sigma_all = jnp.broadcast_to(sigma[:, 0:1], (ny, nz))
 
     def second_image(x, carry):
-        uu, rr, ru, rv, uv = carry
+        rr, ru, rv, uv = carry
         half = H[x]
         wxm, wxp = weights_x(x, half)
         wy, wz, diag = WY[x], WZ[x], D[x]
@@ -350,14 +350,13 @@
             here = U[c, x]
             image = diag * here - inflow(U, c, x, here, wxm, wxp, wy, wz)
             rest = B[c, x] - sigma_all * here
-            uu += fold(here * here)
             rr += fold(rest * rest)
             ru += fold(rest * here)
             rv += fold(rest * image)
             uv += fold(here * image)
-        return uu, rr, ru, rv, uv
-
-    uu, rr, ru, rv, uv = lax.fori_loop(0, nx, second_image, (zero,) * 5)
+        return rr, ru, rv, uv
+
+    rr, ru, rv, uv = lax.fori_loop(0, nx, second_image, (zero,) * 4, unroll=2)
 
     def source_of(field, xlo, xhi, rlo, rhi, out, ylo, yhi):
         def body(x, below, above):
@@ -451,8 +450,7 @@
             out = [a + b for a, b in zip(out, shifted)]
         return out + [sigma, weight]
 
-    weight = everywhere(uu)
-    state = [lanes(m) for m in (uu, rr, ru, rv, uv)] + [sigma, weight]
+    state = [lanes(m) for m in (uu, rr, ru, rv, uv)] + [sigma, total]
 
     def reduce_start(stage, state):
         base = sum(len(s) for s in stages[:stage])
@@ -575,27 +573,27 @@
     block = (nx, ny, nz)
     hbm, vmem = (pl.BlockSpec(memory_space=m) for m in (pltpu.HBM, pltpu.VMEM))
     dma = pltpu.SemaphoreType.DMA
-    scratch = [pltpu.VMEM((3,) + block, f32)]
-    scratch += [pltpu.VMEM(block, t) for t in [f32] * 2 + [jnp.int32] * 3 + [f32] * 4]
+    scratch = [pltpu.VMEM(block, t) for t in [f32] * 2 + [jnp.int32] * 3 + [f32] * 4]
     scratch += [pltpu.VMEM((3,) + block, f32)]
     for fields in (4, 3, 3):
         scratch += [pltpu.VMEM((fields, nx, nz), f32)] * 4
         scratch += [pltpu.VMEM((fields, ny, nz), f32)] * 2
-        if len(scratch) == 11 + 12:
+        if len(scratch) == 10 + 12:
             scratch += [pltpu.VMEM((3, ny, nz), f32)] * 2 + [pltpu.VMEM((3, nx, nz), f32)] * 2
     scratch += [pltpu.VMEM((4, 8, nz), f32)] * 2
     scratch += [pltpu.VMEM((partners + len(GROUPS), 8, 128), f32)]
     scratch += [pltpu.SMEM((4,), f32)] * 3
     scratch += [dma((8,))] + [dma((4,))] * 2 + [dma((6,))] * 2 + [dma((4,))] * 4 + [dma((partners,))] * 2
-    u, t, coef = pl.pallas_call(
+    u, t, coef, b_here = pl.pallas_call(
         functools.partial(kernel, gx_size, gy_size),
         out_shape=(
             jax.ShapeDtypeStruct((3,) + block, f32),
             jax.ShapeDtypeStruct((2,) + block, f32),
             jax.ShapeDtypeStruct((8, 128), f32),
+            jax.ShapeDtypeStruct((3,) + block, f32),
         ),
         in_specs=[hbm] * 8,
-        out_specs=(vmem, vmem, vmem),
+        out_specs=(vmem,) * 4,
         scratch_shapes=scratch,
         compiler_params=pltpu.CompilerParams(
             collective_id=0, has_side_effects=True, vmem_limit_bytes=40 * 1024 * 1024
@@ -614,7 +612,7 @@
         ],
         compiler_params=pltpu.CompilerParams(vmem_limit_bytes=16 * 1024 * 1024),
         name="combine",
-    )(coef, b, u, t)
+    )(coef, b_here, u, t)
 
 
 def solution(mesh):

time: 32.9 us -> 32.3 us (0.982)
  Pallas kernels: 32.2 us -> 31.6 us
    pallas_call x1, Pallas kernels: 30.8 us -> 30.1 us  [per_device(): pl.pallas_call(functools.partial(kernel, gx_size, gy_size), out_shape=(ja...]
where the time goes in v5:
time: 32.3 us; the launch traced here: 32.2 us
  Pallas kernels  31.6 us (98%)
  between operations  0.64 us (2%)
    pallas_call x1, Pallas kernels, per_device(): pl.pallas_call(functools.partial(kernel, gx_size, gy_size), out_shape=(ja...  30.1 us
    pallas_call x1, Pallas kernels, per_device(): pl.pallas_call(combine, out_shape=(jax.ShapeDtypeStruct((3,) + block, f32...  1.45 us

profile of v5, /device:TPU:1, one launch (start us, length us, event | category | flops | bytes accessed | tf_op | source)
XLA Modules:
  0.0 32.2 jit_solution(10504398322825860592)
XLA Ops:
  0.6 30.1 %adjoint.1 = (f32[3,16,16,512]{3,2,1,0:T(8,128)S(1)}, f32[2,16,16,512]{3,2,1,0:T(8,128)S(1)}, f32[8,128]{1,0:T(8,128)S(1)}, f32[3,16,16,512]{3,2,1,0:T(8,128)S(1)}) custom-call(f32[3,16,16,512]{3,2,1,0:T(8,128)} %b_hbm.1, f32[16,16,512]{2,1,0:T(8,128)} %warm_hbm.1, s32[16,16,512]{2,1,0:T(8,128)} %yield_hbm.1, s32[16,16,512]{2,1,0:T(8,128)} %print_hbm.1, ...), custom_call_target="tpu_custom_call" | custom-call | tf_op jit(solution)/shard_map/adjoint/pallas_call | solution.py:587
  30.7 1.4 %combine.1 = (f32[3,16,16,512]{3,2,1,0:T(8,128)}, f32[16,16,512]{2,1,0:T(8,128)}) custom-call(f32[8,128]{1,0:T(8,128)S(1)} %get-tuple-element.6.coef, f32[3,16,16,512]{3,2,1,0:T(8,128)S(1)} %get-tuple-element.7.b, f32[3,16,16,512]{3,2,1,0:T(8,128)S(1)} %get-tuple-element.8.u, f32[2,16,16,512]{3,2,1,0:T(8,128)S(1)} %get-tuple-element.9.t), custom_call_target="tpu_custom_call" | custom-call | tf_op jit(solution)/shard_map/combine/pallas_call | solution.py:603

commit v6 on v5

--- a/solution.py
+++ b/solution.py
@@ -205,10 +205,6 @@
         remote(corner.at[k], rcorner.at[3 - k], send_c.at[k], recv_c.at[3 - k], partner)
         for k, partner in enumerate(diagonal)
     ]
-    for copy, inside in zip(copies_c, inside_c):
-        @pl.when(inside)
-        def _():
-            copy.start()
 
     copies1y = faces_y(y1_lo, y1_hi, ry1_lo, ry1_hi, send1, recv1)
     fields = pl.ds(0, 3)
@@ -225,6 +221,10 @@
     )
     start_faces(*copies1y)
     start_faces(*copies1x)
+    for copy, inside in zip(copies_c, inside_c):
+        @pl.when(inside)
+        def _():
+            copy.start()
 
     def next_y(plane):
         return pltpu.roll(plane, ny - 1, 0)

time: 32.3 us -> 31.8 us (0.985)
  Pallas kernels: 31.6 us -> 31.1 us
    pallas_call x1, Pallas kernels: 30.1 us -> 29.6 us  [per_device(): pl.pallas_call(functools.partial(kernel, gx_size, gy_size), out_shape=(ja...]
where the time goes in v6:
time: 31.8 us; the launch traced here: 31.7 us
  Pallas kernels  31.1 us (98%)
  between operations  0.64 us (2%)
    pallas_call x1, Pallas kernels, per_device(): pl.pallas_call(functools.partial(kernel, gx_size, gy_size), out_shape=(ja...  29.6 us
    pallas_call x1, Pallas kernels, per_device(): pl.pallas_call(combine, out_shape=(jax.ShapeDtypeStruct((3,) + block, f32...  1.45 us

profile of v6, /device:TPU:1, one launch (start us, length us, event | category | flops | bytes accessed | tf_op | source)
XLA Modules:
  0.0 31.7 jit_solution(159091268458836209)
XLA Ops:
  0.6 29.6 %adjoint.1 = (f32[3,16,16,512]{3,2,1,0:T(8,128)S(1)}, f32[2,16,16,512]{3,2,1,0:T(8,128)S(1)}, f32[8,128]{1,0:T(8,128)S(1)}, f32[3,16,16,512]{3,2,1,0:T(8,128)S(1)}) custom-call(f32[3,16,16,512]{3,2,1,0:T(8,128)} %b_hbm.1, f32[16,16,512]{2,1,0:T(8,128)} %warm_hbm.1, s32[16,16,512]{2,1,0:T(8,128)} %yield_hbm.1, s32[16,16,512]{2,1,0:T(8,128)} %print_hbm.1, ...), custom_call_target="tpu_custom_call" | custom-call | tf_op jit(solution)/shard_map/adjoint/pallas_call | solution.py:587
  30.3 1.4 %combine.1 = (f32[3,16,16,512]{3,2,1,0:T(8,128)}, f32[16,16,512]{2,1,0:T(8,128)}) custom-call(f32[8,128]{1,0:T(8,128)S(1)} %get-tuple-element.6.coef, f32[3,16,16,512]{3,2,1,0:T(8,128)S(1)} %get-tuple-element.7.b, f32[3,16,16,512]{3,2,1,0:T(8,128)S(1)} %get-tuple-element.8.u, f32[2,16,16,512]{3,2,1,0:T(8,128)S(1)} %get-tuple-element.9.t), custom_call_target="tpu_custom_call" | custom-call | tf_op jit(solution)/shard_map/combine/pallas_call | solution.py:603
